TPU v7x, 32 devices: a whole 2x2x4 slice. The times are simulated.
32 devices in a mesh: grp: 2 (over y), seq: 4 (over z), head: 2 (over x), rep: 2 (over core).
Axes of the slice: x: 2, y: 2, z: 4, core: 2. Of those that a mesh axis runs over, the one named last changes fastest.
Arguments:
- events: bfloat16 [8192, 512], P(('grp', 'seq', 'rep')), parts along dimension 0, may hold values from -6 to 6
- norm_gain: float32 [512], replicated, may hold values from 0.1 to 1.9
- in_weight: bfloat16 [512, 4, 512], P(None, None, 'head'), may hold values from -0.25 to 0.25
- out_weight: bfloat16 [512, 512], P('head'), may hold values from -0.25 to 0.25
- pair_mask: int32 [16, 4], P(('grp', 'seq', 'rep')), parts along dimension 0, may hold values from 0 to 1, as said below
- cotangent: bfloat16 [8192, 512], P(('grp', 'seq', 'rep')), parts along dimension 0, may hold values from -6 to 6
Outputs:
- output: bfloat16 [8192, 512], P(('grp', 'seq', 'rep')), parts along dimension 0
- grad_events: float32 [8192, 512], P(('grp', 'seq', 'rep')), parts along dimension 0
- grad_in: float32 [1024, 4, 512], P('grp', None, 'head'), parts along dimension 0
- grad_out: float32 [1024, 512], P(('grp', 'head')), parts along dimension 0
- grad_gain: float32 [1024], P('grp'), parts along dimension 0
There are 2 independent parts, one for each index of `grp`. A program takes and returns all parts, laid end to end along the dimension named above; an argument that names none is the same for every part. Nothing has to cross between parts.
Inputs may be any that keep to these rules, and one draw needn't show every extreme that they name: pair_mask[i, r] is 1 where query block i attends key block i + o_r with o = (-2, -1, 1, 2), else 0; it is 0 wherever i + o_r lies outside the 8 blocks.
All inputs are finite; a program needn't handle non-finite values.
Results may differ from a plain program's by a relative error of at most 0.0072.
Values may be sent and summed in bfloat16 or wider, within the bound.
No kernel may reach another device: no remote copies, remote signals or barrier semaphores. Data moves between devices by JAX's collectives and lax.ppermute only.
A program may use at most 64 MiB of HBM per device.

v0:
```python
import functools

import jax
import jax.numpy as jnp
from jax import lax
from jax.experimental import pallas as pl
from jax.experimental.pallas import tpu as pltpu
from jax.sharding import PartitionSpec as P

D = 512
E = 64
BLOCK = 512
CHUNKS = 4
MASK_ROWS = 16
GAIN_ROWS = 16
TOP = 320
LANES = 128
F32 = jnp.float32
BF16 = jnp.bfloat16
VMEM_BYTES = 16 * 1024 * 1024


def dot_nt(a, b):
    return lax.dot_general(a, b, (((1,), (1,)), ((), ())), preferred_element_type=F32)


def dot_tn(a, b):
    return lax.dot_general(a, b, (((0,), (0,)), ((), ())), preferred_element_type=F32)


def dot_nn(a, b):
    return lax.dot_general(a, b, (((1,), (0,)), ((), ())), preferred_element_type=F32)


def sigmoid(x):
    return 0.5 * jnp.tanh(0.5 * x) + 0.5


def whole(shape):
    zeros = (0,) * len(shape)
    return pl.BlockSpec(shape, lambda *_: zeros)


def call(kernel, out_shapes, args, scalars=(), us=0.0, fetched=0):
    n_scalars, n_out = len(scalars), len(out_shapes)

    def with_fetch(*refs):
        head, held, rest = refs[:n_scalars], refs[n_scalars : n_scalars + fetched], refs[n_scalars + fetched :]
        n_rest = len(args) - fetched + n_out
        slots, sems = rest[n_rest : n_rest + fetched], rest[n_rest + fetched]
        copies = [pltpu.make_async_copy(h, slot, sems.at[i]) for i, (h, slot) in enumerate(zip(held, slots))]
        for copy in copies:
            copy.start()

        def fetch(*which):
            for i in which:
                copies[i].wait()

        kernel(*head, *slots, *rest[:n_rest], fetch)

    scratch = [pltpu.VMEM(a.shape, a.dtype) for a in args[:fetched]]
    return pl.pallas_call(
        with_fetch if fetched else kernel,
        out_shape=out_shapes,
        in_specs=[pl.BlockSpec(memory_space=pltpu.SMEM)] * n_scalars
        + [pl.BlockSpec(memory_space=pltpu.HBM)] * fetched
        + [pl.BlockSpec(memory_space=pltpu.VMEM)] * (len(args) - fetched),
        out_specs=[pl.BlockSpec(memory_space=pltpu.VMEM)] * n_out,
        scratch_shapes=scratch + [pltpu.SemaphoreType.DMA((fetched,))] if fetched else [],
        compiler_params=pltpu.CompilerParams(vmem_limit_bytes=VMEM_BYTES),
        cost_estimate=pl.CostEstimate(flops=int(us * 1.1e9), bytes_accessed=0, transcendentals=0),
    )(*scalars, *args)


def shape(dims, dtype):
    return jax.ShapeDtypeStruct(dims, dtype)


def mask_at(where, mask_own, mask_oth, slot, col):
    at = jnp.where(where[1] == 1, col, 3 - col)
    return jnp.where(where[0] == slot, mask_own[0, at], mask_oth[0, at])


def slots(where):
    mine = where[0]
    return [pl.ds(pl.multiple_of(slot * BLOCK, BLOCK), BLOCK) for slot in (mine, 1 - mine)]


def project_kv_kernel(where, ev_own, ev_oth, w4, gain, normed, inv, slope, kv, fetch):
    fetch(0, 2)
    w_kv = jnp.concatenate([w4[2], w4[3]], axis=1)
    for i, (rows, events) in enumerate(zip(slots(where), (ev_own, ev_oth))):
        if i == 1:
            fetch(1)
        x = events[...].astype(F32)
        inverse = lax.rsqrt(jnp.mean(x * x, axis=1, keepdims=True) + 1e-06)
        n = (x * inverse * gain[...]).astype(BF16)
        normed[rows, :] = n
        inv[rows, :] = jnp.broadcast_to(inverse, (BLOCK, LANES))
        p = dot_nn(n, w_kv)
        s = sigmoid(p)
        slope[rows, :] = s * (1.0 + p * (1.0 - s))
        kv[rows, :] = (p * s).astype(BF16)


def project_gq_kernel(where, mask_own, mask_oth, cot_own, cot_oth, w4, ow, normed, slope, qa, gate, gm, fetch):
    w = w4.shape[2]
    fetch(0, 2, 3)
    w_gq = jnp.concatenate([w4[0], w4[1]], axis=1)
    wow = ow[pl.ds(pl.multiple_of(where[3] * w, w), w), :]
    for i, (rows, cot) in enumerate(zip(slots(where), (cot_own, cot_oth))):
        if i == 1:
            fetch(1)
        p = dot_nn(normed[rows, :], w_gq)
        s = sigmoid(p)
        slope[rows, :] = s * (1.0 + p * (1.0 - s))
        act = (p * s).astype(BF16)
        g = act[:, :w]
        gate[rows, :] = g
        grad_mixed = dot_nt(cot[...], wow)
        gm[rows, :] = grad_mixed
        qa[rows, :w] = act[:, w:]
        qa[rows, w:] = (grad_mixed * g.astype(F32)).astype(BF16)
    lane = lax.broadcasted_iota(jnp.int32, (MASK_ROWS, 2 * w), 1)
    marks = jnp.zeros((MASK_ROWS, 2 * w), F32)
    for slot in range(2):
        for col in range(4):
            m = mask_at(where, mask_own, mask_oth, slot, col).astype(F32)
            marks = jnp.where(lane == 4 * slot + col, m, marks)
    qa[2 * BLOCK :, :] = marks.astype(BF16)


TILE = 512


def block_rows(slot):
    return pl.ds(pl.multiple_of(slot * BLOCK, BLOCK), BLOCK)


def pair_side(left, l_slot, right, r_slot, acc):
    w = left.shape[1] // 2
    rows, r_rows = block_rows(l_slot), block_rows(r_slot)
    xr, yr = right[r_rows, :w], right[r_rows, w:]
    lane = lax.broadcasted_iota(jnp.int32, (1, w), 1) // E
    zero = jnp.zeros_like(xr)
    x = left[rows, :w] * jnp.asarray(0.5, BF16)
    y = left[rows, w:]
    acc_x = acc[rows, :w]
    acc_y = acc[rows, w:]
    for h in range(w // E):
        on = lane == h
        xh, yh = jnp.where(on, xr, zero), jnp.where(on, yr, zero)
        u = dot_nt(x, xh)
        g = dot_nt(y, yh)
        a = 1.0 + jnp.tanh(u)
        m = u * a
        slope = a + m * (2.0 - a)
        acc_y = acc_y + dot_nn(m.astype(BF16), yh)
        acc_x = acc_x + dot_nn((g * slope).astype(BF16), xh)
    acc[rows, :w] = acc_x
    acc[rows, w:] = acc_y


def pair_both(qa, q_slot, kv, k_slot, acc_q, acc_k):
    w = qa.shape[1] // 2
    k_rows = block_rows(k_slot)
    k, v = kv[k_rows, :w], kv[k_rows, w:]
    lane = lax.broadcasted_iota(jnp.int32, (1, w), 1) // E
    zero = jnp.zeros_like(k)
    grad_k, grad_v = acc_k[k_rows, :w], acc_k[k_rows, w:]
    for t in range(BLOCK // TILE):
        rows = pl.ds(pl.multiple_of(q_slot * BLOCK + t * TILE, TILE), TILE)
        q = qa[rows, :w] * jnp.asarray(0.5, BF16)
        ga = qa[rows, w:]
        acc_x = acc_q[rows, :w]
        acc_y = acc_q[rows, w:]
        for h in range(w // E):
            on = lane == h
            kh, vh = jnp.where(on, k, zero), jnp.where(on, v, zero)
            u = dot_nt(q, kh)
            a = 1.0 + jnp.tanh(u)
            m = u * a
            slope = a + m * (2.0 - a)
            weights = m.astype(BF16)
            grad_s = (dot_nt(ga, vh) * slope).astype(BF16)
            acc_y = acc_y + dot_nn(weights, vh)
            acc_x = acc_x + dot_nn(grad_s, kh)
            grad_k = grad_k + 2.0 * dot_tn(grad_s, jnp.where(on, q, jnp.zeros_like(q)))
            grad_v = grad_v + dot_tn(weights, jnp.where(on, ga, jnp.zeros_like(ga)))
        acc_q[rows, :w] = acc_x
        acc_q[rows, w:] = acc_y
    acc_k[k_rows, :w] = grad_k
    acc_k[k_rows, w:] = grad_v


def remote_pair(t, odd):
    q_slot, k_slot = (t == 1).astype(jnp.int32), (t == 2).astype(jnp.int32)
    col = 2 + (t > 0).astype(jnp.int32)
    return (1 - q_slot, 1 - k_slot, 3 - col) if odd else (q_slot, k_slot, col)


def loop(count, step):
    lax.fori_loop(0, count, lambda t, _: (step(t), 0)[1], 0)


def query_kernel(odd, where, mask_own, mask_oth, qa, kv, acc):
    acc[...] = jnp.zeros_like(acc)

    def step(t):
        q_slot, k_slot, col = remote_pair(t, odd)

        @pl.when(mask_at(where, mask_own, mask_oth, q_slot, col) == 1)
        def _():
            pair_side(qa, q_slot, kv, k_slot, acc)

    loop(3, step)


def key_kernel(odd, where, kv, qa, acc):
    acc[...] = jnp.zeros_like(acc)
    marks = qa[2 * BLOCK :, :].astype(F32)
    row = lax.broadcasted_iota(jnp.int32, marks.shape, 0)
    lane = lax.broadcasted_iota(jnp.int32, marks.shape, 1)

    def step(t):
        q_slot, k_slot, col = remote_pair(t, odd)
        m = jnp.sum(jnp.where((row == 0) & (lane == 4 * q_slot + col), marks, 0.0))
        on = m > 0.5
        if odd:
            on = on & (where[2] == 0)

        @pl.when(on)
        def _():
            pair_side(kv, k_slot, qa, q_slot, acc)

    loop(3, step)


def own_kernel(where, mask_own, mask_oth, qa, kv, normed, acc_q, acc_k, normed_t):
    normed_t[...] = normed[...].T
    acc_q[...] = jnp.zeros_like(acc_q)
    acc_k[...] = jnp.zeros_like(acc_k)

    def step(t):
        q_slot = t % 2
        k_slot = ((t == 1) | (t == 2)).astype(jnp.int32)
        masked = mask_at(where, mask_own, mask_oth, q_slot, jnp.maximum(t - 1, 0))

        @pl.when((t < 2) | (masked == 1))
        def _():
            pair_both(qa, q_slot, kv, k_slot, acc_q, acc_k)

    loop(4, step)


def query_finish_kernel(where, cot_own, cot_oth, gate, gm, slopes, normed_t, acc_a, acc_b, acc_c, mix_own, mix_oth, gp, packed):
    w = gate.shape[1]
    grad_out = jnp.zeros((w, D), F32)
    for rows, cot, mixed in zip(slots(where), (cot_own, cot_oth), (mix_own, mix_oth)):
        total = acc_a[rows, :] + acc_b[rows, :] + acc_c[rows, :]
        grad_query = total[:, :w] * (1.0 / 1024)
        attended = total[:, w:] * (1.0 / 512)
        mix = (attended * gate[rows, :].astype(F32)).astype(BF16)
        mixed[...] = mix
        slope = slopes[rows, :]
        gp[rows, :w] = (gm[rows, :] * attended * slope[:, :w]).astype(BF16)
        gp[rows, w:] = (grad_query * slope[:, w:]).astype(BF16)
        grad_out = grad_out + dot_tn(mix, cot[...])
    pack(packed, dot_nn(normed_t[...], gp[...]), grad_out)


def pack(packed, grad_in, grad_out=None):
    step = D // CHUNKS
    w = grad_in.shape[1] // 2
    for c in range(CHUNKS):
        for p in range(2):
            packed[c, p * step : (p + 1) * step, :] = grad_in[c * step : (c + 1) * step, p * w : (p + 1) * w].astype(BF16)
        if grad_out is not None:
            n = w // CHUNKS
            part = grad_out[c * n : (c + 1) * n].astype(BF16)
            for j in range(D // w):
                packed[c, 2 * step + j * n : 2 * step + (j + 1) * n, :] = part[:, j * w : (j + 1) * w]


def key_finish_kernel(
    where, ev_own, ev_oth, inv, slopes, normed_t, gp_gq, w4, acc_a, acc_b, acc_c, packed, gn_own, gn_oth, gp
):
    w = slopes.shape[1] // 2
    w_gq = jnp.concatenate([w4[0], w4[1]], axis=1)
    w_kv = jnp.concatenate([w4[2], w4[3]], axis=1)
    gain = jnp.zeros((1, D), F32)
    for rows, events, out in zip(slots(where), (ev_own, ev_oth), (gn_own, gn_oth)):
        total = acc_a[rows, :] + acc_b[rows, :] + acc_c[rows, :]
        slope = slopes[rows, :]
        gp[rows, :w] = (total[:, :w] * (1.0 / 1024) * slope[:, :w]).astype(BF16)
        gp[rows, w:] = (total[:, w:] * (1.0 / 512) * slope[:, w:]).astype(BF16)
        gn = dot_nt(gp_gq[rows, :], w_gq) + dot_nt(gp[rows, :], w_kv)
        out[...] = gn.astype(BF16)
        inverse = jnp.concatenate([inv[rows, :]] * (D // LANES), axis=1)
        gain = gain + jnp.sum(gn * events[...].astype(F32) * inverse, axis=0, keepdims=True)
    pack(packed, dot_nn(normed_t[...], gp[...]))
    high = gain.astype(BF16).astype(F32)
    parts = [v[:, j * w : (j + 1) * w] for v in (high, gain - high) for j in range(D // w)]
    if len(parts) < GAIN_ROWS:
        parts.append(jnp.zeros((GAIN_ROWS - len(parts), w), F32))
    for c in range(CHUNKS):
        packed[c, D // CHUNKS * 2 :, :] = jnp.concatenate(parts, axis=0).astype(BF16)


def add_cores_kernel(order, a, b, top, bottom):
    total = (a[...].astype(F32) + b[...].astype(F32)).astype(BF16)
    top[...] = total[:TOP]
    bottom[...] = total[TOP:]


def add_chunks_gain_kernel(order, *refs):
    pieces, (bottom, out, wide) = refs[:4], refs[4:]
    n, w = out.shape
    a, b, c, d = (piece[...].astype(F32) for piece in pieces)
    total = (a + b) + (c + d)
    out[...] = total[:n].astype(BF16)
    k = D // w
    rows = [total[n + j : n + j + 1] + total[n + k + j : n + k + j + 1] for j in range(k)]
    gain = jnp.concatenate(rows, axis=1)
    wide[: BLOCK - TOP, :] = bottom[...]
    wide[BLOCK - TOP :, :] = split_rows(gain)


def split_rows(total):
    high = total.astype(BF16).astype(F32)
    rest = jnp.zeros((GAIN_ROWS - 2, total.shape[1]), F32)
    return jnp.concatenate([high, total - high, rest], axis=0).astype(BF16)


def join_rows(rows):
    both = rows.astype(F32)
    return both[0:1] + both[1:2]


def add_chunks_kernel(order, a, b, c, d, out):
    out[...] = ((a[...].astype(F32) + b[...].astype(F32)) + (c[...].astype(F32) + d[...].astype(F32))).astype(BF16)


def assemble_kernel(first, where, *refs):
    pieces, rest = refs[:8], refs[8:]
    if first:
        pg_a, pg_b, _, grad_in, pg, parts, sem = rest
        pg[...] = pg_a[...] + pg_b[...]
    else:
        grad_in, grad_out, parts, sem = rest
    w = pieces[0].shape[1]
    step = D // CHUNKS
    n = w // CHUNKS

    def place(i, piece, core):
        lanes = slice(core * w, (core + 1) * w)
        rows = pl.ds(pl.multiple_of(where[4 + i] * step, step), step)
        for p in range(2):
            parts[p, rows, lanes] = piece[p * step : (p + 1) * step, :].astype(F32)
        if first == 0:
            for j in range(D // w):
                block = piece[2 * step + j * n : 2 * step + (j + 1) * n, :]
                out_rows = pl.ds(pl.multiple_of(core * w + where[4 + i] * n, n), n)
                grad_out[out_rows, j * w : (j + 1) * w] = block.astype(F32)

    def copy(i, p):
        rows = pl.ds(pl.multiple_of(where[4 + i] * step, step), step)
        return pltpu.make_async_copy(parts.at[p, rows], grad_in.at[rows, first + p], sem.at[i, p])

    for i in range(CHUNKS):
        for core in range(2):

            @pl.when(where[3] == core)
            def _():
                place(i, pieces[i], core)
                place(i, pieces[4 + i], 1 - core)

        for p in range(2):
            copy(i, p).start()
    for i in range(CHUNKS):
        for p in range(2):
            copy(i, p).wait()


def events_kernel(events, gain, top, bottom, top_x, bottom_x, grad, pg):
    for start, rows, mine, other in ((0, TOP, top, top_x), (TOP, BLOCK - TOP, bottom, bottom_x)):
        x = events[start : start + rows, :].astype(F32)
        inverse = lax.rsqrt(jnp.mean(x * x, axis=1, keepdims=True) + 1e-06)
        gn = mine[:rows, :].astype(F32) + other[:rows, :].astype(F32)
        scaled = gn * gain[...]
        mean = jnp.mean(scaled * x, axis=1, keepdims=True)
        grad[start : start + rows, :] = inverse * scaled - x * (inverse * inverse * inverse) * mean
    pg[...] = join_rows(bottom[BLOCK - TOP :, :]) + join_rows(bottom_x[BLOCK - TOP :, :])


def output_kernel(where, mine, rep, mine_x, rep_x, ow, ow_x, out):
    w = mine.shape[1]
    r = where[3]
    first = pl.ds(pl.multiple_of(r * w, w), w)
    second = pl.ds(pl.multiple_of((1 - r) * w, w), w)
    here = dot_nn(mine[...], ow[first, :]) + dot_nn(rep[...], ow[second, :])
    there = dot_nn(mine_x[...], ow_x[first, :]) + dot_nn(rep_x[...], ow_x[second, :])
    out[...] = (here + there).astype(BF16)


def swap(x, axis, bit=1):
    n = lax.axis_size(axis)
    return lax.ppermute(x, axis, [(i, i ^ bit) for i in range(n)])


def route_even(n):
    return [(2 * i + r, 2 * (i ^ 1) + r) for i in range(n) for r in range(2)]


def route_odd(n):
    route = []
    for i in range(n):
        for r in range(2):
            if i in (0, n - 1):
                route.append((2 * i + r, 2 * i + 1 - r))
            else:
                route.append((2 * i + r, 2 * (((i - 1) ^ 1) + 1) + r))
    return route


def scatter_over_seq(packed):
    me = lax.axis_index("seq")

    def chunk(d):
        return lax.dynamic_index_in_dim(packed, me ^ d, 0, keepdims=False)

    return [chunk(0)] + [swap(chunk(d), "seq", d) for d in (1, 2, 3)]


def gather_over_seq(total):
    return [total] + [swap(total, "seq", d) for d in (1, 2, 3)]


def after(values, *others):
    return lax.optimization_barrier((values, others))[0]


def body(events, norm_gain, in_weight, out_weight, pair_mask, cotangent):
    n_seq, n_head = lax.axis_size("seq"), lax.axis_size("head")
    direct = n_seq == CHUNKS and n_head == 2
    rep, seq = lax.axis_index("rep"), lax.axis_index("seq")
    w = in_weight.shape[2] // 2
    rows2 = 2 * BLOCK
    step = D // CHUNKS
    flip = 1 - seq % 2
    edge = ((seq == 0) | (seq == n_seq - 1)).astype(jnp.int32)
    chunk_ids = [(seq ^ d) if direct else jnp.int32(d) for d in range(CHUNKS)]
    where = jnp.stack([rep ^ flip, flip, edge, rep] + chunk_ids).astype(jnp.int32)

    ev_oth = swap(events, "rep")
    cot_oth = swap(cotangent, "rep")
    mask_oth = swap(pair_mask, "rep")
    scalars = [where, pair_mask, mask_oth]
    gain = norm_gain.reshape(1, D)
    w4 = lax.dynamic_slice(in_weight, (0, 0, rep * w), (D, 4, w)).transpose(1, 0, 2)
    axes = ("seq", "rep")
    even, odd = route_even(n_seq), route_odd(n_seq)

    normed, inv, slope_kv, kv = call(
        project_kv_kernel,
        [shape((rows2, D), BF16), shape((rows2, LANES), F32), shape((rows2, 2 * w), F32), shape((rows2, 2 * w), BF16)],
        [events, ev_oth, w4, gain],
        [where],
        fetched=3,
    )
    kv_even = lax.ppermute(kv, axes, even)
    kv_odd = lax.ppermute(kv, axes, odd)
    slope_gq, qa, gate, gm = call(
        project_gq_kernel,
        [
            shape((rows2, 2 * w), F32),
            shape((rows2 + MASK_ROWS, 2 * w), BF16),
            shape((rows2, w), BF16),
            shape((rows2, w), F32),
        ],
        [cotangent, cot_oth, w4, out_weight, normed],
        scalars,
        fetched=4,
    )
    qa_even = lax.ppermute(qa, axes, even)
    qa_odd = lax.ppermute(qa, axes, odd)
    acc_shape = shape((rows2, 2 * w), F32)
    q_own, k_own, normed_t = call(
        own_kernel, [acc_shape, acc_shape, shape((D, rows2), BF16)], [qa, kv, normed], scalars, us=9
    )
    (q_even,) = call(functools.partial(query_kernel, False), [acc_shape], [qa, kv_even], scalars, us=5)
    late = where
    if n_head == 2:
        ow_x = swap(out_weight, "head")
        late = after(where, ow_x, q_even)
    (q_odd,) = call(
        functools.partial(query_kernel, True), [acc_shape], [qa, kv_odd], [late, pair_mask, mask_oth], us=5
    )
    mix_own, mix_oth, gp_gq, pack_q = call(
        query_finish_kernel,
        [
            shape((BLOCK, w), BF16),
            shape((BLOCK, w), BF16),
            shape((rows2, 2 * w), BF16),
            shape((CHUNKS, 2 * step + D // CHUNKS, w), BF16),
        ],
        [cotangent, cot_oth, gate, gm, slope_gq, normed_t, q_own, q_even, q_odd],
        [where],
    )
    mix_rep = swap(mix_oth, "rep")
    (k_far,) = call(functools.partial(key_kernel, False), [acc_shape], [kv, qa_even], [where], us=6)
    add_shape = shape((2 * step + D // CHUNKS, w), BF16)
    if direct:
        mixed_x = [swap(mix_own, "head"), swap(mix_rep, "head")]
        got_q = scatter_over_seq(pack_q)
        late = after(where, k_far, got_q)
        (sum_q,) = call(add_chunks_kernel, [add_shape], got_q, [where])
        all_q = gather_over_seq(sum_q)
    else:
        mixed_x = []
        late = where
        sums = lax.psum(pack_q.astype(F32), "seq").astype(BF16)
        all_q = [sums[i] for i in range(CHUNKS)]
    (k_last,) = call(functools.partial(key_kernel, True), [acc_shape], [kv, qa_odd], [late], us=6)
    oth_q = [swap(piece, "rep") for piece in all_q]
    last = after(where, k_last, mixed_x, all_q)

    pack_kv, gn_own, gn_oth, _ = call(
        key_finish_kernel,
        [
            shape((CHUNKS, 2 * step + GAIN_ROWS, w), BF16),
            shape((BLOCK, D), BF16),
            shape((BLOCK, D), BF16),
            shape((rows2, 2 * w), BF16),
        ],
        [events, ev_oth, inv, slope_kv, normed_t, gp_gq, w4, k_own, k_far, k_last],
        [last],
    )
    late = where
    if direct:
        got_kv = scatter_over_seq(pack_kv)
    halves = [shape((TOP, D), BF16), shape((BLOCK - TOP, D), BF16)]
    top, bottom = call(add_cores_kernel, halves, [gn_own, swap(gn_oth, "rep")], [late])
    if n_head == 2:
        (output,) = call(
            output_kernel,
            [shape((BLOCK, D), BF16)],
            [mix_own, mix_rep, *(mixed_x or [swap(mix_own, "head"), swap(mix_rep, "head")]), out_weight, ow_x],
            [where],
        )
        top_x = swap(top, "head")
    else:
        weight = jnp.where(rep == 0, out_weight, jnp.roll(out_weight, w, axis=0))
        mixed = jnp.concatenate([mix_own, mix_rep], axis=1)
        output = lax.psum(dot_nn(mixed, weight), "head").astype(BF16)
        top, bottom = lax.psum((top.astype(F32), bottom.astype(F32)), "head")
        top_x = jnp.zeros_like(top)
    wide = shape((BLOCK - TOP + GAIN_ROWS, D), BF16)
    if direct:
        sum_kv, bottom = call(
            add_chunks_gain_kernel,
            [shape((2 * step, w), BF16), wide],
            [*got_kv, bottom],
            [after(where, output, oth_q)],
        )
        bottom_x = swap(bottom, "head")
        all_kv = gather_over_seq(sum_kv)
    else:
        sums = lax.psum(pack_kv.astype(F32), "seq")
        all_kv = [sums[i, : 2 * step].astype(BF16) for i in range(CHUNKS)]
        pg = sums[0, 2 * step :]
        pg = (pg[: D // w] + pg[D // w : 2 * (D // w)]).reshape(1, D)
        pg = jnp.concatenate([pg, jnp.zeros((GAIN_ROWS - 1, D), F32)])
        bottom, bottom_x = jnp.concatenate([bottom, lax.psum(pg, "head")]), jnp.zeros(wide.shape, F32)
    grad_events, pg = call(
        events_kernel,
        [shape((BLOCK, D), F32), shape((1, D), F32)],
        [events, gain, top, bottom, top_x, bottom_x],
    )
    grad_in, grad_out = assemble(late, [*all_q, *oth_q], w)
    all_kv = after(all_kv, grad_out, pg)
    oth_kv = [swap(piece, "rep") for piece in all_kv]
    grad_in, pg = assemble(where, [*all_kv, *oth_kv, pg, swap(pg, "rep")], w, grad_in)
    return (output, grad_events, grad_in, grad_out, pg.reshape(D))


def assemble(where, pieces, w, grad_in=None):
    held = [] if grad_in is None else [grad_in]
    hbm, vmem = pl.BlockSpec(memory_space=pltpu.HBM), pl.BlockSpec(memory_space=pltpu.VMEM)
    return pl.pallas_call(
        functools.partial(assemble_kernel, 2 * len(held)),
        out_shape=[shape((D, 4, 2 * w), F32), shape((1, D) if held else (2 * w, D), F32)],
        in_specs=[pl.BlockSpec(memory_space=pltpu.SMEM)] + [vmem] * len(pieces) + [hbm] * len(held),
        out_specs=[hbm, vmem],
        input_output_aliases={1 + len(pieces): 0} if held else {},
        scratch_shapes=[pltpu.VMEM((2, D, 2 * w), F32), pltpu.SemaphoreType.DMA((CHUNKS, 2))],
        compiler_params=pltpu.CompilerParams(vmem_limit_bytes=VMEM_BYTES),
        cost_estimate=pl.CostEstimate(flops=0, bytes_accessed=0, transcendentals=0),
    )(where, *pieces, *held)


def solution(mesh):
    return jax.shard_map(
        body,
        mesh=mesh,
        in_specs=(
            P(("grp", "seq", "rep"), None),
            P(),
            P(None, None, "head"),
            P("head", None),
            P(("grp", "seq", "rep"), None),
            P(("grp", "seq", "rep"), None),
        ),
        out_specs=(
            P(("grp", "seq", "rep"), None),
            P(("grp", "seq", "rep"), None),
            P("grp", None, "head"),
            P(("grp", "head"), None),
            P("grp"),
        ),
        check_vma=False,
    )
```

profile of v0, /device:TPU:0, one launch (start us, length us, event | category | flops | bytes accessed | tf_op | source)
XLA Modules:
  0.0 89.2 jit_solution(11434105181470386573)
XLA Ops:
  1.7 2.6 %collective-permute-start.4 = (bf16[256,512]{1,0:T(8,128)(2,1)}, bf16[256,512]{1,0:T(8,128)(2,1)}, u32[]{:S(2)}, u32[]{:S(2)}) collective-permute-start(bf16[256,512]{1,0:T(8,128)(2,1)} %ow.1), channel_id=1, source_target_pairs={{0,2},{2,0},{1,3},{3,1},{4,6},{6,4},{5,7},{7,5},{8,10},{10,8},{9,1... | collective-permute-start | bytes 786440 | tf_op jit(solution)/shard_map/ppermute | solution.py:408
  4.7 2.2 %shard_map.101 = (bf16[1024,512]{1,0:T(8,128)(2,1)S(1)}, f32[1024,128]{1,0:T(8,128)S(1)}, f32[1024,256]{1,0:T(8,128)S(1)}, bf16[1024,256]{1,0:T(8,128)(2,1)S(1)}) custom-call(s32[8]{0:T(128)S(1)} %stack.39.refs_0_.where.order, bf16[512,512]{1,0:T(8,128)(2,1)S(1)} %copy-done.1, bf16[512,512]{1,0:T(8,128)(2,1)} %collective-permute-done.2.refs_2_.ev_oth, ...), custom_call_target="tpu_custom_call" | custom-call | tf_op jit(solution)/shard_map/pallas_call | solution.py:62
  6.9 1.6 %collective-permute-start.3 = (bf16[1024,256]{1,0:T(8,128)(2,1)S(1)}, bf16[1024,256]{1,0:T(8,128)(2,1)S(1)}, u32[]{:S(2)}, u32[]{:S(2)}) collective-permute-start(bf16[1024,256]{1,0:T(8,128)(2,1)S(1)} %get-tuple-element.46.kv), channel_id=1, source_target_pairs={{0,4},{1,5},{4,0},{5,1},{8,12},{9,13},{12,8},{13,9},{2,6},{3,7},{6... | collective-permute-start | bytes 1572872 | tf_op jit(solution)/shard_map/ppermute | solution.py:471
  8.6 1.8 %shard_map.102 = (f32[1024,256]{1,0:T(8,128)S(1)}, bf16[1040,256]{1,0:T(8,128)(2,1)S(1)}, bf16[1024,128]{1,0:T(8,128)(2,1)S(1)}, f32[1024,128]{1,0:T(8,128)S(1)}) custom-call(s32[8]{0:T(128)S(1)} %stack.39.refs_0_.where.order, s32[1,4]{1,0:T(1,128)S(1)} %copy-done.5, s32[1,4]{1,0:T(1,128)S(1)} %collective-permute-done.1.refs_2_.mask_oth, ...), custom_call_target="tpu_custom_call" | custom-call | tf_op jit(solution)/shard_map/pallas_call | solution.py:62
  10.3 3.2 %collective-permute-start.9 = (bf16[1040,256]{1,0:T(8,128)(2,1)S(1)}, bf16[1040,256]{1,0:T(8,128)(2,1)S(1)}, u32[]{:S(2)}, u32[]{:S(2)}) collective-permute-start(bf16[1040,256]{1,0:T(8,128)(2,1)S(1)} %get-tuple-element.45.qa), channel_id=1, source_target_pairs={{0,4},{1,5},{4,0},{5,1},{8,12},{9,13},{12,8},{13,9},{2,6},{3,7},{6... | collective-permute-start | bytes 1597448 | tf_op jit(solution)/shard_map/ppermute | solution.py:485
  13.6 7.6 %shard_map.103 = (f32[1024,256]{1,0:T(8,128)S(1)}, f32[1024,256]{1,0:T(8,128)S(1)}, bf16[512,1024]{1,0:T(8,128)(2,1)S(1)}) custom-call(s32[8]{0:T(128)S(1)} %stack.39.refs_0_.where.order, s32[1,4]{1,0:T(1,128)S(1)} %copy-done.5, s32[1,4]{1,0:T(1,128)S(1)} %collective-permute-done.1.refs_2_.mask_oth, bf16[1040,256]{1,0:T(8,128)(2,1)S(1)} %get-tuple-element.45.qa, ...), custom_call_target="tpu_custom_call" | custom-call | flops 9900000256 | tf_op jit(solution)/shard_map/pallas_call | solution.py:62
  21.7 3.6 %shard_map.104.acc_b = f32[1024,256]{1,0:T(8,128)S(1)} custom-call(s32[8]{0:T(128)S(1)} %stack.39.refs_0_.where.order, s32[1,4]{1,0:T(1,128)S(1)} %copy-done.5, s32[1,4]{1,0:T(1,128)S(1)} %collective-permute-done.1.refs_2_.mask_oth, bf16[1040,256]{1,0:T(8,128)(2,1)S(1)} %get-tuple-element.45.qa, bf16[1024,256]{1,0:T(8,128)(2,1)S(1)} %collective-permute-done.3.kv), custom_call_target="tpu_custom_call" | custom-call | flops 5500000256 | tf_op jit(solution)/shard_map/pallas_call | solution.py:62
  26.0 1.5 %shard_map.106 = (bf16[512,128]{1,0:T(8,128)(2,1)S(1)}, bf16[512,128]{1,0:T(8,128)(2,1)S(1)}, bf16[1024,256]{1,0:T(8,128)(2,1)S(1)}, bf16[4,384,128]{2,1,0:T(8,128)(2,1)S(1)}) custom-call(s32[8]{0:T(128)S(1)} %stack.39.refs_0_.where.order, bf16[512,512]{1,0:T(8,128)(2,1)S(1)} %copy-done.2, bf16[512,512]{1,0:T(8,128)(2,1)S(1)} %collective-permute-done.refs_4_.cot_oth, ...), custom_call_target="tpu_custom_call" | custom-call | tf_op jit(solution)/shard_map/pallas_call | solution.py:62
  27.6 3.1 %collective-permute-start.10 = (bf16[384,128]{1,0:T(8,128)(2,1)S(1)}, bf16[384,128]{1,0:T(8,128)(2,1)S(1)}, u32[]{:S(2)}, u32[]{:S(2)}) collective-permute-start(bf16[384,128]{1,0:T(8,128)(2,1)S(1)} %get-tuple-element.79), channel_id=1, source_target_pairs={{0,4},{4,0},{8,12},{12,8},{1,5},{5,1},{9,13},{13,9},{2,6},{6,2},{1... | collective-permute-start | bytes 294920 | tf_op jit(solution)/shard_map/ppermute | solution.py:408
  30.7 6.1 %collective-permute-start.11 = (bf16[384,128]{1,0:T(8,128)(2,1)S(1)}, bf16[384,128]{1,0:T(8,128)(2,1)S(1)}, u32[]{:S(2)}, u32[]{:S(2)}) collective-permute-start(bf16[384,128]{1,0:T(8,128)(2,1)S(1)} %get-tuple-element.78), channel_id=1, source_target_pairs={{0,8},{4,12},{8,0},{12,4},{1,9},{5,13},{9,1},{13,5},{2,10},{6,14},... | collective-permute-start | bytes 294920 | tf_op jit(solution)/shard_map/ppermute | solution.py:408
  36.8 1.4 %collective-permute-start.12 = (bf16[384,128]{1,0:T(8,128)(2,1)S(1)}, bf16[384,128]{1,0:T(8,128)(2,1)S(1)}, u32[]{:S(2)}, u32[]{:S(2)}) collective-permute-start(bf16[384,128]{1,0:T(8,128)(2,1)S(1)} %get-tuple-element.77), channel_id=1, source_target_pairs={{0,12},{4,8},{8,4},{12,0},{1,13},{5,9},{9,5},{13,1},{2,14},{6,10},... | collective-permute-start | bytes 294920 | tf_op jit(solution)/shard_map/ppermute | solution.py:408
  38.2 3.9 %shard_map.108.acc_b = f32[1024,256]{1,0:T(8,128)S(1)} custom-call(s32[8]{0:T(128)S(1)} %stack.39.refs_0_.where.order, bf16[1024,256]{1,0:T(8,128)(2,1)S(1)} %get-tuple-element.46.kv, bf16[1040,256]{1,0:T(8,128)(2,1)S(1)} %collective-permute-done.9.qa), custom_call_target="tpu_custom_call" | custom-call | flops 6600000000 | tf_op jit(solution)/shard_map/pallas_call | solution.py:62
  42.1 1.3 %collective-permute-start.7 = (bf16[512,128]{1,0:T(8,128)(2,1)S(1)}, bf16[512,128]{1,0:T(8,128)(2,1)S(1)}, u32[]{:S(2)}, u32[]{:S(2)}) collective-permute-start(bf16[512,128]{1,0:T(8,128)(2,1)S(1)} %get-tuple-element.50.mine), channel_id=1, source_target_pairs={{0,2},{2,0},{1,3},{3,1},{4,6},{6,4},{5,7},{7,5},{8,10},{10,8},{9,1... | collective-permute-start | bytes 393224 | tf_op jit(solution)/shard_map/ppermute | solution.py:408
  45.1 1.9 %collective-permute-start.14 = (bf16[384,128]{1,0:T(8,128)(2,1)S(1)}, bf16[384,128]{1,0:T(8,128)(2,1)S(1)}, u32[]{:S(2)}, u32[]{:S(2)}) collective-permute-start(bf16[384,128]{1,0:T(8,128)(2,1)S(1)} %shard_map.110.refs_0_), channel_id=1, source_target_pairs={{0,4},{4,0},{8,12},{12,8},{1,5},{5,1},{9,13},{13,9},{2,6},{6,2},{1... | collective-permute-start | bytes 294920 | tf_op jit(solution)/shard_map/ppermute | solution.py:408
  46.9 1.9 %collective-permute-start.15 = (bf16[384,128]{1,0:T(8,128)(2,1)S(1)}, bf16[384,128]{1,0:T(8,128)(2,1)S(1)}, u32[]{:S(2)}, u32[]{:S(2)}) collective-permute-start(bf16[384,128]{1,0:T(8,128)(2,1)S(1)} %shard_map.110.refs_0_), channel_id=1, source_target_pairs={{0,8},{4,12},{8,0},{12,4},{1,9},{5,13},{9,1},{13,5},{2,10},{6,14},... | collective-permute-start | bytes 294920 | tf_op jit(solution)/shard_map/ppermute | solution.py:408
  48.8 1.4 %collective-permute-start.16 = (bf16[384,128]{1,0:T(8,128)(2,1)S(1)}, bf16[384,128]{1,0:T(8,128)(2,1)S(1)}, u32[]{:S(2)}, u32[]{:S(2)}) collective-permute-start(bf16[384,128]{1,0:T(8,128)(2,1)S(1)} %shard_map.110.refs_0_), channel_id=1, source_target_pairs={{0,12},{4,8},{8,4},{12,0},{1,13},{5,9},{9,5},{13,1},{2,14},{6,10},... | collective-permute-start | bytes 294920 | tf_op jit(solution)/shard_map/ppermute | solution.py:408
  50.2 1.2 %collective-permute-start.8 = (bf16[512,128]{1,0:T(8,128)(2,1)S(1)}, bf16[512,128]{1,0:T(8,128)(2,1)S(1)}, u32[]{:S(2)}, u32[]{:S(2)}) collective-permute-start(bf16[512,128]{1,0:T(8,128)(2,1)S(1)} %collective-permute-done.6.rep), channel_id=1, source_target_pairs={{0,2},{2,0},{1,3},{3,1},{4,6},{6,4},{5,7},{7,5},{8,10},{10,8},{9,1... | collective-permute-start | bytes 393224 | tf_op jit(solution)/shard_map/ppermute | solution.py:408
  51.4 1.2 %shard_map.109.acc_c = f32[1024,256]{1,0:T(8,128)S(1)} custom-call(s32[8]{0:T(128)S(1)} %stack.39.refs_0_.where.order, bf16[1024,256]{1,0:T(8,128)(2,1)S(1)} %get-tuple-element.46.kv, bf16[1040,256]{1,0:T(8,128)(2,1)S(1)} %collective-permute-done.13.qa), custom_call_target="tpu_custom_call" | custom-call | flops 6600000000 | tf_op jit(solution)/shard_map/pallas_call | solution.py:62
  53.8 3.4 %collective-permute-done.16.refs_3_ = bf16[384,128]{1,0:T(8,128)(2,1)S(1)} collective-permute-done((bf16[384,128]{1,0:T(8,128)(2,1)S(1)}, bf16[384,128]{1,0:T(8,128)(2,1)S(1)}, u32[]{:S(2)}, u32[]{:S(2)}) %collective-permute-start.16) | collective-permute-done | bytes 98336 | tf_op jit(solution)/shard_map/ppermute | solution.py:408
  57.2 2.3 %shard_map.111 = (bf16[4,272,128]{2,1,0:T(8,128)(2,1)S(1)}, bf16[512,512]{1,0:T(8,128)(2,1)S(1)}, bf16[512,512]{1,0:T(8,128)(2,1)S(1)}, bf16[1024,256]{1,0:T(8,128)(2,1)}) custom-call(s32[8]{0:T(128)S(1)} %stack.39.refs_0_.where.order, bf16[512,512]{1,0:T(8,128)(2,1)S(1)} %copy-done.1, bf16[512,512]{1,0:T(8,128)(2,1)} %collective-permute-done.2.refs_2_.ev_oth, ...), custom_call_target="tpu_custom_call" | custom-call | tf_op jit(solution)/shard_map/pallas_call | solution.py:62
  62.2 1.3 %collective-permute-start.25 = (bf16[320,512]{1,0:T(8,128)(2,1)S(1)}, bf16[320,512]{1,0:T(8,128)(2,1)S(1)}, u32[]{:S(2)}, u32[]{:S(2)}) collective-permute-start(bf16[320,512]{1,0:T(8,128)(2,1)S(1)} %get-tuple-element.61.top), channel_id=1, source_target_pairs={{0,2},{2,0},{1,3},{3,1},{4,6},{6,4},{5,7},{7,5},{8,10},{10,8},{9,1... | collective-permute-start | bytes 983048 | tf_op jit(solution)/shard_map/ppermute | solution.py:408
  63.5 2.3 %collective-permute-start.22 = (bf16[272,128]{1,0:T(8,128)(2,1)S(1)}, bf16[272,128]{1,0:T(8,128)(2,1)S(1)}, u32[]{:S(2)}, u32[]{:S(2)}) collective-permute-start(bf16[272,128]{1,0:T(8,128)(2,1)S(1)} %get-tuple-element.83), channel_id=1, source_target_pairs={{0,4},{4,0},{8,12},{12,8},{1,5},{5,1},{9,13},{13,9},{2,6},{6,2},{1... | collective-permute-start | bytes 208904 | tf_op jit(solution)/shard_map/ppermute | solution.py:408
  65.8 1.5 %collective-permute-start.23 = (bf16[272,128]{1,0:T(8,128)(2,1)S(1)}, bf16[272,128]{1,0:T(8,128)(2,1)S(1)}, u32[]{:S(2)}, u32[]{:S(2)}) collective-permute-start(bf16[272,128]{1,0:T(8,128)(2,1)S(1)} %get-tuple-element.82), channel_id=1, source_target_pairs={{0,8},{4,12},{8,0},{12,4},{1,9},{5,13},{9,1},{13,5},{2,10},{6,14},... | collective-permute-start | bytes 208904 | tf_op jit(solution)/shard_map/ppermute | solution.py:408
  67.3 1.4 %collective-permute-start.24 = (bf16[272,128]{1,0:T(8,128)(2,1)S(1)}, bf16[272,128]{1,0:T(8,128)(2,1)S(1)}, u32[]{:S(2)}, u32[]{:S(2)}) collective-permute-start(bf16[272,128]{1,0:T(8,128)(2,1)S(1)} %get-tuple-element.81), channel_id=1, source_target_pairs={{0,12},{4,8},{8,4},{12,0},{1,13},{5,9},{9,5},{13,1},{2,14},{6,10},... | collective-permute-start | bytes 208904 | tf_op jit(solution)/shard_map/ppermute | solution.py:408
  68.8 2.4 %shard_map.107 = bf16[512,512]{1,0:T(8,128)(2,1)} custom-call(s32[8]{0:T(128)S(1)} %stack.39.refs_0_.where.order, bf16[512,128]{1,0:T(8,128)(2,1)S(1)} %get-tuple-element.50.mine, bf16[512,128]{1,0:T(8,128)(2,1)S(1)} %collective-permute-done.6.rep, bf16[512,128]{1,0:T(8,128)(2,1)S(1)} %collective-permute-done.7.mine_x, ...), custom_call_target="tpu_custom_call" | custom-call | tf_op jit(solution)/shard_map/pallas_call | solution.py:62
  71.2 3.0 %collective-permute-done.23.refs_2_ = bf16[272,128]{1,0:T(8,128)(2,1)S(1)} collective-permute-done((bf16[272,128]{1,0:T(8,128)(2,1)S(1)}, bf16[272,128]{1,0:T(8,128)(2,1)S(1)}, u32[]{:S(2)}, u32[]{:S(2)}) %collective-permute-start.23) | collective-permute-done | bytes 69664 | tf_op jit(solution)/shard_map/ppermute | solution.py:408
  75.6 1.5 %collective-permute-start.27 = (bf16[256,128]{1,0:T(8,128)(2,1)S(1)}, bf16[256,128]{1,0:T(8,128)(2,1)S(1)}, u32[]{:S(2)}, u32[]{:S(2)}) collective-permute-start(bf16[256,128]{1,0:T(8,128)(2,1)S(1)} %get-tuple-element.70.refs_0_), channel_id=1, source_target_pairs={{0,4},{4,0},{8,12},{12,8},{1,5},{5,1},{9,13},{13,9},{2,6},{6,2},{1... | collective-permute-start | bytes 196616 | tf_op jit(solution)/shard_map/ppermute | solution.py:408
  77.1 1.3 %collective-permute-start.28 = (bf16[256,128]{1,0:T(8,128)(2,1)S(1)}, bf16[256,128]{1,0:T(8,128)(2,1)S(1)}, u32[]{:S(2)}, u32[]{:S(2)}) collective-permute-start(bf16[256,128]{1,0:T(8,128)(2,1)S(1)} %get-tuple-element.70.refs_0_), channel_id=1, source_target_pairs={{0,8},{4,12},{8,0},{12,4},{1,9},{5,13},{9,1},{13,5},{2,10},{6,14},... | collective-permute-start | bytes 196616 | tf_op jit(solution)/shard_map/ppermute | solution.py:408
  78.5 1.6 %collective-permute-start.29 = (bf16[256,128]{1,0:T(8,128)(2,1)S(1)}, bf16[256,128]{1,0:T(8,128)(2,1)S(1)}, u32[]{:S(2)}, u32[]{:S(2)}) collective-permute-start(bf16[256,128]{1,0:T(8,128)(2,1)S(1)} %get-tuple-element.70.refs_0_), channel_id=1, source_target_pairs={{0,12},{4,8},{8,4},{12,0},{1,13},{5,9},{9,5},{13,1},{2,14},{6,10},... | collective-permute-start | bytes 196616 | tf_op jit(solution)/shard_map/ppermute | solution.py:408
  80.0 2.4 %shard_map.115 = (f32[512,4,256]{2,1,0:T(4,128)}, f32[256,512]{1,0:T(8,128)}) custom-call(s32[8]{0:T(128)S(1)} %stack.39.refs_0_.where.order, bf16[384,128]{1,0:T(8,128)(2,1)S(1)} %shard_map.110.refs_0_, bf16[384,128]{1,0:T(8,128)(2,1)S(1)} %collective-permute-done.14.refs_1_, bf16[384,128]{1,0:T(8,128)(2,1)S(1)} %collective-permute-done.15.refs_2_, ...), custom_call_target="tpu_custom_call" | custom-call | tf_op jit(solution)/shard_map/pallas_call | solution.py:590
  82.5 1.5 %shard_map.114 = (f32[512,512]{1,0:T(8,128)}, f32[1,512]{1,0:T(1,128)S(1)}) custom-call(bf16[512,512]{1,0:T(8,128)(2,1)S(1)} %copy-done.1, f32[1,512]{1,0:T(1,128)S(1)} %bitcast.33, bf16[320,512]{1,0:T(8,128)(2,1)S(1)} %get-tuple-element.61.top, bf16[208,512]{1,0:T(8,128)(2,1)S(1)} %get-tuple-element.65.bottom, ...), custom_call_target="tpu_custom_call" | custom-call | tf_op jit(solution)/shard_map/pallas_call | solution.py:62
  86.9 2.2 %shard_map.116 = (f32[512,4,256]{2,1,0:T(4,128)}, f32[1,512]{1,0:T(1,128)}) custom-call(s32[8]{0:T(128)S(1)} %stack.39.refs_0_.where.order, bf16[256,128]{1,0:T(8,128)(2,1)S(1)} %get-tuple-element.70.refs_0_, bf16[256,128]{1,0:T(8,128)(2,1)S(1)} %collective-permute-done.27.refs_1_, ...), custom_call_target="tpu_custom_call", output_to_operand_aliasing={{0}: (11, {})} | custom-call | tf_op jit(solution)/shard_map/pallas_call | solution.py:590
  (71 shorter events, 12.5 us)
Async XLA Ops:
  0.7 4.0 %collective-permute-start.2 = (bf16[512,512]{1,0:T(8,128)(2,1)}, bf16[512,512]{1,0:T(8,128)(2,1)}, u32[]{:S(2)}, u32[]{:S(2)}) collective-permute-start(bf16[512,512]{1,0:T(8,128)(2,1)} %events.1), channel_id=1, source_target_pairs={{0,1},{1,0},{2,3},{3,2},{4,5},{5,4},{6,7},{7,6},{8,9},{9,8},{10,11... | collective-permute-start | bytes 1572872 | tf_op jit(solution)/shard_map/ppermute | solution.py:408
  1.2 7.3 %collective-permute-start = (bf16[512,512]{1,0:T(8,128)(2,1)}, bf16[512,512]{1,0:T(8,128)(2,1)S(1)}, u32[]{:S(2)}, u32[]{:S(2)}) collective-permute-start(bf16[512,512]{1,0:T(8,128)(2,1)} %cot_own.1), channel_id=1, source_target_pairs={{0,1},{1,0},{2,3},{3,2},{4,5},{5,4},{6,7},{7,6},{8,9},{9,8},{10,11... | collective-permute-start | bytes 1572872 | tf_op jit(solution)/shard_map/ppermute | solution.py:408
  1.3 7.2 %collective-permute-start.1 = (s32[1,4]{1,0:T(1,128)}, s32[1,4]{1,0:T(1,128)S(1)}, u32[]{:S(2)}, u32[]{:S(2)}) collective-permute-start(s32[1,4]{1,0:T(1,128)} %mask_own.5), channel_id=1, source_target_pairs={{0,1},{1,0},{2,3},{3,2},{4,5},{5,4},{6,7},{7,6},{8,9},{9,8},{10,11... | collective-permute-start | bytes 56 | tf_op jit(solution)/shard_map/ppermute | solution.py:408
  1.7 23.6 %collective-permute-start.4 = (bf16[256,512]{1,0:T(8,128)(2,1)}, bf16[256,512]{1,0:T(8,128)(2,1)}, u32[]{:S(2)}, u32[]{:S(2)}) collective-permute-start(bf16[256,512]{1,0:T(8,128)(2,1)} %ow.1), channel_id=1, source_target_pairs={{0,2},{2,0},{1,3},{3,1},{4,6},{6,4},{5,7},{7,5},{8,10},{10,8},{9,1... | collective-permute-start | bytes 786440 | tf_op jit(solution)/shard_map/ppermute | solution.py:408
  6.9 14.8 %collective-permute-start.3 = (bf16[1024,256]{1,0:T(8,128)(2,1)S(1)}, bf16[1024,256]{1,0:T(8,128)(2,1)S(1)}, u32[]{:S(2)}, u32[]{:S(2)}) collective-permute-start(bf16[1024,256]{1,0:T(8,128)(2,1)S(1)} %get-tuple-element.46.kv), channel_id=1, source_target_pairs={{0,4},{1,5},{4,0},{5,1},{8,12},{9,13},{12,8},{13,9},{2,6},{3,7},{6... | collective-permute-start | bytes 1572872 | tf_op jit(solution)/shard_map/ppermute | solution.py:471
  8.5 16.8 %collective-permute-start.5 = (bf16[1024,256]{1,0:T(8,128)(2,1)S(1)}, bf16[1024,256]{1,0:T(8,128)(2,1)S(1)}, u32[]{:S(2)}, u32[]{:S(2)}) collective-permute-start(bf16[1024,256]{1,0:T(8,128)(2,1)S(1)} %get-tuple-element.46.kv), channel_id=1, source_target_pairs={{0,1},{1,0},{4,8},{5,9},{8,4},{9,5},{12,13},{13,12},{2,3},{3,2},{6... | collective-permute-start | bytes 1572872 | tf_op jit(solution)/shard_map/ppermute | solution.py:472
  10.3 27.8 %collective-permute-start.9 = (bf16[1040,256]{1,0:T(8,128)(2,1)S(1)}, bf16[1040,256]{1,0:T(8,128)(2,1)S(1)}, u32[]{:S(2)}, u32[]{:S(2)}) collective-permute-start(bf16[1040,256]{1,0:T(8,128)(2,1)S(1)} %get-tuple-element.45.qa), channel_id=1, source_target_pairs={{0,4},{1,5},{4,0},{5,1},{8,12},{9,13},{12,8},{13,9},{2,6},{3,7},{6... | collective-permute-start | bytes 1597448 | tf_op jit(solution)/shard_map/ppermute | solution.py:485
  13.6 35.3 %collective-permute-start.13 = (bf16[1040,256]{1,0:T(8,128)(2,1)S(1)}, bf16[1040,256]{1,0:T(8,128)(2,1)S(1)}, u32[]{:S(2)}, u32[]{:S(2)}) collective-permute-start(bf16[1040,256]{1,0:T(8,128)(2,1)S(1)} %get-tuple-element.45.qa), channel_id=1, source_target_pairs={{0,1},{1,0},{4,8},{5,9},{8,4},{9,5},{12,13},{13,12},{2,3},{3,2},{6... | collective-permute-start | bytes 1597448 | tf_op jit(solution)/shard_map/ppermute | solution.py:486
  27.6 14.5 %collective-permute-start.10 = (bf16[384,128]{1,0:T(8,128)(2,1)S(1)}, bf16[384,128]{1,0:T(8,128)(2,1)S(1)}, u32[]{:S(2)}, u32[]{:S(2)}) collective-permute-start(bf16[384,128]{1,0:T(8,128)(2,1)S(1)} %get-tuple-element.79), channel_id=1, source_target_pairs={{0,4},{4,0},{8,12},{12,8},{1,5},{5,1},{9,13},{13,9},{2,6},{6,2},{1... | collective-permute-start | bytes 294920 | tf_op jit(solution)/shard_map/ppermute | solution.py:408
  30.7 12.7 %collective-permute-start.11 = (bf16[384,128]{1,0:T(8,128)(2,1)S(1)}, bf16[384,128]{1,0:T(8,128)(2,1)S(1)}, u32[]{:S(2)}, u32[]{:S(2)}) collective-permute-start(bf16[384,128]{1,0:T(8,128)(2,1)S(1)} %get-tuple-element.78), channel_id=1, source_target_pairs={{0,8},{4,12},{8,0},{12,4},{1,9},{5,13},{9,1},{13,5},{2,10},{6,14},... | collective-permute-start | bytes 294920 | tf_op jit(solution)/shard_map/ppermute | solution.py:408
  36.8 7.7 %collective-permute-start.12 = (bf16[384,128]{1,0:T(8,128)(2,1)S(1)}, bf16[384,128]{1,0:T(8,128)(2,1)S(1)}, u32[]{:S(2)}, u32[]{:S(2)}) collective-permute-start(bf16[384,128]{1,0:T(8,128)(2,1)S(1)} %get-tuple-element.77), channel_id=1, source_target_pairs={{0,12},{4,8},{8,4},{12,0},{1,13},{5,9},{9,5},{13,1},{2,14},{6,10},... | collective-permute-start | bytes 294920 | tf_op jit(solution)/shard_map/ppermute | solution.py:408
  38.2 12.0 %collective-permute-start.6 = (bf16[512,128]{1,0:T(8,128)(2,1)S(1)}, bf16[512,128]{1,0:T(8,128)(2,1)S(1)}, u32[]{:S(2)}, u32[]{:S(2)}) collective-permute-start(bf16[512,128]{1,0:T(8,128)(2,1)S(1)} %get-tuple-element.51), channel_id=1, source_target_pairs={{0,1},{1,0},{2,3},{3,2},{4,5},{5,4},{6,7},{7,6},{8,9},{9,8},{10,11... | collective-permute-start | bytes 393224 | tf_op jit(solution)/shard_map/ppermute | solution.py:408
  42.1 10.5 %collective-permute-start.7 = (bf16[512,128]{1,0:T(8,128)(2,1)S(1)}, bf16[512,128]{1,0:T(8,128)(2,1)S(1)}, u32[]{:S(2)}, u32[]{:S(2)}) collective-permute-start(bf16[512,128]{1,0:T(8,128)(2,1)S(1)} %get-tuple-element.50.mine), channel_id=1, source_target_pairs={{0,2},{2,0},{1,3},{3,1},{4,6},{6,4},{5,7},{7,5},{8,10},{10,8},{9,1... | collective-permute-start | bytes 393224 | tf_op jit(solution)/shard_map/ppermute | solution.py:408
  45.1 7.6 %collective-permute-start.14 = (bf16[384,128]{1,0:T(8,128)(2,1)S(1)}, bf16[384,128]{1,0:T(8,128)(2,1)S(1)}, u32[]{:S(2)}, u32[]{:S(2)}) collective-permute-start(bf16[384,128]{1,0:T(8,128)(2,1)S(1)} %shard_map.110.refs_0_), channel_id=1, source_target_pairs={{0,4},{4,0},{8,12},{12,8},{1,5},{5,1},{9,13},{13,9},{2,6},{6,2},{1... | collective-permute-start | bytes 294920 | tf_op jit(solution)/shard_map/ppermute | solution.py:408
  46.9 6.8 %collective-permute-start.15 = (bf16[384,128]{1,0:T(8,128)(2,1)S(1)}, bf16[384,128]{1,0:T(8,128)(2,1)S(1)}, u32[]{:S(2)}, u32[]{:S(2)}) collective-permute-start(bf16[384,128]{1,0:T(8,128)(2,1)S(1)} %shard_map.110.refs_0_), channel_id=1, source_target_pairs={{0,8},{4,12},{8,0},{12,4},{1,9},{5,13},{9,1},{13,5},{2,10},{6,14},... | collective-permute-start | bytes 294920 | tf_op jit(solution)/shard_map/ppermute | solution.py:408
  48.8 8.4 %collective-permute-start.16 = (bf16[384,128]{1,0:T(8,128)(2,1)S(1)}, bf16[384,128]{1,0:T(8,128)(2,1)S(1)}, u32[]{:S(2)}, u32[]{:S(2)}) collective-permute-start(bf16[384,128]{1,0:T(8,128)(2,1)S(1)} %shard_map.110.refs_0_), channel_id=1, source_target_pairs={{0,12},{4,8},{8,4},{12,0},{1,13},{5,9},{9,5},{13,1},{2,14},{6,10},... | collective-permute-start | bytes 294920 | tf_op jit(solution)/shard_map/ppermute | solution.py:408
  50.2 7.0 %collective-permute-start.8 = (bf16[512,128]{1,0:T(8,128)(2,1)S(1)}, bf16[512,128]{1,0:T(8,128)(2,1)S(1)}, u32[]{:S(2)}, u32[]{:S(2)}) collective-permute-start(bf16[512,128]{1,0:T(8,128)(2,1)S(1)} %collective-permute-done.6.rep), channel_id=1, source_target_pairs={{0,2},{2,0},{1,3},{3,1},{4,6},{6,4},{5,7},{7,5},{8,10},{10,8},{9,1... | collective-permute-start | bytes 393224 | tf_op jit(solution)/shard_map/ppermute | solution.py:408
  59.6 2.0 %collective-permute-start.17 = (bf16[512,512]{1,0:T(8,128)(2,1)S(1)}, bf16[512,512]{1,0:T(8,128)(2,1)S(1)}, u32[]{:S(2)}, u32[]{:S(2)}) collective-permute-start(bf16[512,512]{1,0:T(8,128)(2,1)S(1)} %get-tuple-element.60), channel_id=1, source_target_pairs={{0,1},{1,0},{2,3},{3,2},{4,5},{5,4},{6,7},{7,6},{8,9},{9,8},{10,11... | collective-permute-start | bytes 1572872 | tf_op jit(solution)/shard_map/ppermute | solution.py:408
  59.6 3.9 %collective-permute-start.18 = (bf16[384,128]{1,0:T(8,128)(2,1)S(1)}, bf16[384,128]{1,0:T(8,128)(2,1)S(1)}, u32[]{:S(2)}, u32[]{:S(2)}) collective-permute-start(bf16[384,128]{1,0:T(8,128)(2,1)S(1)} %shard_map.110.refs_0_), channel_id=1, source_target_pairs={{0,1},{1,0},{2,3},{3,2},{4,5},{5,4},{6,7},{7,6},{8,9},{9,8},{10,11... | collective-permute-start | bytes 294920 | tf_op jit(solution)/shard_map/ppermute | solution.py:408
  60.1 5.7 %collective-permute-start.19 = (bf16[384,128]{1,0:T(8,128)(2,1)S(1)}, bf16[384,128]{1,0:T(8,128)(2,1)S(1)}, u32[]{:S(2)}, u32[]{:S(2)}) collective-permute-start(bf16[384,128]{1,0:T(8,128)(2,1)S(1)} %collective-permute-done.14.refs_1_), channel_id=1, source_target_pairs={{0,1},{1,0},{2,3},{3,2},{4,5},{5,4},{6,7},{7,6},{8,9},{9,8},{10,11... | collective-permute-start | bytes 294920 | tf_op jit(solution)/shard_map/ppermute | solution.py:408
  60.2 7.1 %collective-permute-start.20 = (bf16[384,128]{1,0:T(8,128)(2,1)S(1)}, bf16[384,128]{1,0:T(8,128)(2,1)S(1)}, u32[]{:S(2)}, u32[]{:S(2)}) collective-permute-start(bf16[384,128]{1,0:T(8,128)(2,1)S(1)} %collective-permute-done.15.refs_2_), channel_id=1, source_target_pairs={{0,1},{1,0},{2,3},{3,2},{4,5},{5,4},{6,7},{7,6},{8,9},{9,8},{10,11... | collective-permute-start | bytes 294920 | tf_op jit(solution)/shard_map/ppermute | solution.py:408
  60.7 10.6 %collective-permute-start.21 = (bf16[384,128]{1,0:T(8,128)(2,1)S(1)}, bf16[384,128]{1,0:T(8,128)(2,1)S(1)}, u32[]{:S(2)}, u32[]{:S(2)}) collective-permute-start(bf16[384,128]{1,0:T(8,128)(2,1)S(1)} %collective-permute-done.16.refs_3_), channel_id=1, source_target_pairs={{0,1},{1,0},{2,3},{3,2},{4,5},{5,4},{6,7},{7,6},{8,9},{9,8},{10,11... | collective-permute-start | bytes 294920 | tf_op jit(solution)/shard_map/ppermute | solution.py:408
  62.2 20.2 %collective-permute-start.25 = (bf16[320,512]{1,0:T(8,128)(2,1)S(1)}, bf16[320,512]{1,0:T(8,128)(2,1)S(1)}, u32[]{:S(2)}, u32[]{:S(2)}) collective-permute-start(bf16[320,512]{1,0:T(8,128)(2,1)S(1)} %get-tuple-element.61.top), channel_id=1, source_target_pairs={{0,2},{2,0},{1,3},{3,1},{4,6},{6,4},{5,7},{7,5},{8,10},{10,8},{9,1... | collective-permute-start | bytes 983048 | tf_op jit(solution)/shard_map/ppermute | solution.py:408
  63.5 7.7 %collective-permute-start.22 = (bf16[272,128]{1,0:T(8,128)(2,1)S(1)}, bf16[272,128]{1,0:T(8,128)(2,1)S(1)}, u32[]{:S(2)}, u32[]{:S(2)}) collective-permute-start(bf16[272,128]{1,0:T(8,128)(2,1)S(1)} %get-tuple-element.83), channel_id=1, source_target_pairs={{0,4},{4,0},{8,12},{12,8},{1,5},{5,1},{9,13},{13,9},{2,6},{6,2},{1... | collective-permute-start | bytes 208904 | tf_op jit(solution)/shard_map/ppermute | solution.py:408
  65.8 8.4 %collective-permute-start.23 = (bf16[272,128]{1,0:T(8,128)(2,1)S(1)}, bf16[272,128]{1,0:T(8,128)(2,1)S(1)}, u32[]{:S(2)}, u32[]{:S(2)}) collective-permute-start(bf16[272,128]{1,0:T(8,128)(2,1)S(1)} %get-tuple-element.82), channel_id=1, source_target_pairs={{0,8},{4,12},{8,0},{12,4},{1,9},{5,13},{9,1},{13,5},{2,10},{6,14},... | collective-permute-start | bytes 208904 | tf_op jit(solution)/shard_map/ppermute | solution.py:408
  67.3 6.9 %collective-permute-start.24 = (bf16[272,128]{1,0:T(8,128)(2,1)S(1)}, bf16[272,128]{1,0:T(8,128)(2,1)S(1)}, u32[]{:S(2)}, u32[]{:S(2)}) collective-permute-start(bf16[272,128]{1,0:T(8,128)(2,1)S(1)} %get-tuple-element.81), channel_id=1, source_target_pairs={{0,12},{4,8},{8,4},{12,0},{1,13},{5,9},{9,5},{13,1},{2,14},{6,10},... | collective-permute-start | bytes 208904 | tf_op jit(solution)/shard_map/ppermute | solution.py:408
  74.8 7.7 %collective-permute-start.26 = (bf16[208,512]{1,0:T(8,128)(2,1)S(1)}, bf16[208,512]{1,0:T(8,128)(2,1)S(1)}, u32[]{:S(2)}, u32[]{:S(2)}) collective-permute-start(bf16[208,512]{1,0:T(8,128)(2,1)S(1)} %get-tuple-element.65.bottom), channel_id=1, source_target_pairs={{0,2},{2,0},{1,3},{3,1},{4,6},{6,4},{5,7},{7,5},{8,10},{10,8},{9,1... | collective-permute-start | bytes 638984 | tf_op jit(solution)/shard_map/ppermute | solution.py:408
  75.6 8.3 %collective-permute-start.27 = (bf16[256,128]{1,0:T(8,128)(2,1)S(1)}, bf16[256,128]{1,0:T(8,128)(2,1)S(1)}, u32[]{:S(2)}, u32[]{:S(2)}) collective-permute-start(bf16[256,128]{1,0:T(8,128)(2,1)S(1)} %get-tuple-element.70.refs_0_), channel_id=1, source_target_pairs={{0,4},{4,0},{8,12},{12,8},{1,5},{5,1},{9,13},{13,9},{2,6},{6,2},{1... | collective-permute-start | bytes 196616 | tf_op jit(solution)/shard_map/ppermute | solution.py:408
  77.1 7.6 %collective-permute-start.28 = (bf16[256,128]{1,0:T(8,128)(2,1)S(1)}, bf16[256,128]{1,0:T(8,128)(2,1)S(1)}, u32[]{:S(2)}, u32[]{:S(2)}) collective-permute-start(bf16[256,128]{1,0:T(8,128)(2,1)S(1)} %get-tuple-element.70.refs_0_), channel_id=1, source_target_pairs={{0,8},{4,12},{8,0},{12,4},{1,9},{5,13},{9,1},{13,5},{2,10},{6,14},... | collective-permute-start | bytes 196616 | tf_op jit(solution)/shard_map/ppermute | solution.py:408
  78.5 6.2 %collective-permute-start.29 = (bf16[256,128]{1,0:T(8,128)(2,1)S(1)}, bf16[256,128]{1,0:T(8,128)(2,1)S(1)}, u32[]{:S(2)}, u32[]{:S(2)}) collective-permute-start(bf16[256,128]{1,0:T(8,128)(2,1)S(1)} %get-tuple-element.70.refs_0_), channel_id=1, source_target_pairs={{0,12},{4,8},{8,4},{12,0},{1,13},{5,9},{9,5},{13,1},{2,14},{6,10},... | collective-permute-start | bytes 196616 | tf_op jit(solution)/shard_map/ppermute | solution.py:408
  84.7 2.2 %collective-permute-start.30 = (bf16[256,128]{1,0:T(8,128)(2,1)S(1)}, bf16[256,128]{1,0:T(8,128)(2,1)S(1)}, u32[]{:S(2)}, u32[]{:S(2)}) collective-permute-start(bf16[256,128]{1,0:T(8,128)(2,1)S(1)} %get-tuple-element.70.refs_0_), channel_id=1, source_target_pairs={{0,1},{1,0},{2,3},{3,2},{4,5},{5,4},{6,7},{7,6},{8,9},{9,8},{10,11... | collective-permute-start | bytes 196616 | tf_op jit(solution)/shard_map/ppermute | solution.py:408
  84.7 2.2 %collective-permute-start.31 = (bf16[256,128]{1,0:T(8,128)(2,1)S(1)}, bf16[256,128]{1,0:T(8,128)(2,1)S(1)}, u32[]{:S(2)}, u32[]{:S(2)}) collective-permute-start(bf16[256,128]{1,0:T(8,128)(2,1)S(1)} %collective-permute-done.27.refs_1_), channel_id=1, source_target_pairs={{0,1},{1,0},{2,3},{3,2},{4,5},{5,4},{6,7},{7,6},{8,9},{9,8},{10,11... | collective-permute-start | bytes 196616 | tf_op jit(solution)/shard_map/ppermute | solution.py:408
  (9 other events, 39.9 us)
where the time goes:
time: 89.1 us; the launch traced here: 89.2 us
  starting transfers between devices  40.6 us (46%)
  Pallas kernels  35.2 us (40%)
  waiting for transfers between devices  11.8 us (13%)
  between operations  1.13 us (1%)
    ppermute x31, starting transfers between devices, swap(): return lax.ppermute(x, axis, [(i, i ^ bit) for i in range(n)])  35.8 us
    pallas_call x14, Pallas kernels, call(): pl.pallas_call(with_fetch if fetched else kernel, out_shape=out_shapes, i...  30.6 us
    ppermute x31, waiting for transfers between devices, swap(): return lax.ppermute(x, axis, [(i, i ^ bit) for i in range(n)])  11.3 us
    pallas_call x2, Pallas kernels, assemble(): pl.pallas_call(functools.partial(assemble_kernel, 2 * len(held)), out_sha...  4.6 us
    ppermute x1, starting transfers between devices, body(): qa_even = lax.ppermute(qa, axes, even)  3.21 us
  transfers between devices with their start and end apart: 35, of which 8 were waited for; matrix products, arithmetic and copies ran while one was open for 0% of the time, Pallas kernels for 34%

commit v1 on v0

--- a/solution.py
+++ b/solution.py
@@ -13,7 +13,6 @@
 CHUNKS = 4
 MASK_ROWS = 16
 GAIN_ROWS = 16
-TOP = 320
 LANES = 128
 F32 = jnp.float32
 BF16 = jnp.bfloat16
@@ -282,13 +281,13 @@
                 packed[c, 2 * step + j * n : 2 * step + (j + 1) * n, :] = part[:, j * w : (j + 1) * w]
 
 
-def key_finish_kernel(
-    where, ev_own, ev_oth, inv, slopes, normed_t, gp_gq, w4, acc_a, acc_b, acc_c, packed, gn_own, gn_oth, gp
+def grad_normed_kernel(
+    where, ev_own, ev_oth, inv, slopes, gp_gq, w4, acc_a, acc_b, acc_c, gn_own, gn_oth, gp, gain
 ):
     w = slopes.shape[1] // 2
     w_gq = jnp.concatenate([w4[0], w4[1]], axis=1)
     w_kv = jnp.concatenate([w4[2], w4[3]], axis=1)
-    gain = jnp.zeros((1, D), F32)
+    share = jnp.zeros((1, D), F32)
     for rows, events, out in zip(slots(where), (ev_own, ev_oth), (gn_own, gn_oth)):
         total = acc_a[rows, :] + acc_b[rows, :] + acc_c[rows, :]
         slope = slopes[rows, :]
@@ -297,44 +296,35 @@
         gn = dot_nt(gp_gq[rows, :], w_gq) + dot_nt(gp[rows, :], w_kv)
         out[...] = gn.astype(BF16)
         inverse = jnp.concatenate([inv[rows, :]] * (D // LANES), axis=1)
-        gain = gain + jnp.sum(gn * events[...].astype(F32) * inverse, axis=0, keepdims=True)
+        share = share + jnp.sum(gn * events[...].astype(F32) * inverse, axis=0, keepdims=True)
+    gain[...] = share
+
+
+def key_weights_kernel(normed_t, gp, gain, packed):
+    w = gp.shape[1] // 2
     pack(packed, dot_nn(normed_t[...], gp[...]))
-    high = gain.astype(BF16).astype(F32)
-    parts = [v[:, j * w : (j + 1) * w] for v in (high, gain - high) for j in range(D // w)]
+    share = gain[...]
+    high = share.astype(BF16).astype(F32)
+    parts = [v[:, j * w : (j + 1) * w] for v in (high, share - high) for j in range(D // w)]
     if len(parts) < GAIN_ROWS:
         parts.append(jnp.zeros((GAIN_ROWS - len(parts), w), F32))
     for c in range(CHUNKS):
         packed[c, D // CHUNKS * 2 :, :] = jnp.concatenate(parts, axis=0).astype(BF16)
 
 
-def add_cores_kernel(order, a, b, top, bottom):
-    total = (a[...].astype(F32) + b[...].astype(F32)).astype(BF16)
-    top[...] = total[:TOP]
-    bottom[...] = total[TOP:]
+def add_cores_kernel(order, a, b, out):
+    out[...] = (a[...].astype(F32) + b[...].astype(F32)).astype(BF16)
 
 
 def add_chunks_gain_kernel(order, *refs):
-    pieces, (bottom, out, wide) = refs[:4], refs[4:]
+    pieces, (out, gain) = refs[:4], refs[4:]
     n, w = out.shape
     a, b, c, d = (piece[...].astype(F32) for piece in pieces)
     total = (a + b) + (c + d)
     out[...] = total[:n].astype(BF16)
     k = D // w
-    rows = [total[n + j : n + j + 1] + total[n + k + j : n + k + j + 1] for j in range(k)]
-    gain = jnp.concatenate(rows, axis=1)
-    wide[: BLOCK - TOP, :] = bottom[...]
-    wide[BLOCK - TOP :, :] = split_rows(gain)
-
-
-def split_rows(total):
-    high = total.astype(BF16).astype(F32)
-    rest = jnp.zeros((GAIN_ROWS - 2, total.shape[1]), F32)
-    return jnp.concatenate([high, total - high, rest], axis=0).astype(BF16)
-
-
-def join_rows(rows):
-    both = rows.astype(F32)
-    return both[0:1] + both[1:2]
+    for j in range(k):
+        gain[:, j * w : (j + 1) * w] = total[n + j : n + j + 1] + total[n + k + j : n + k + j + 1]
 
 
 def add_chunks_kernel(order, a, b, c, d, out):
@@ -342,12 +332,13 @@
 
 
 def assemble_kernel(first, where, *refs):
-    pieces, rest = refs[:8], refs[8:]
     if first:
-        pg_a, pg_b, _, grad_in, pg, parts, sem = rest
+        pieces, (pg_a, pg_b, _, grad_in, pg, parts, sem) = refs[:8], refs[8:]
         pg[...] = pg_a[...] + pg_b[...]
     else:
-        grad_in, grad_out, parts, sem = rest
+        both, (grad_in, grad_out, parts, sem) = refs[:2], refs[2:]
+        n = both[0].shape[0] // CHUNKS
+        pieces = [held.at[pl.ds(i * n, n)] for held in both for i in range(CHUNKS)]
     w = pieces[0].shape[1]
     step = D // CHUNKS
     n = w // CHUNKS
@@ -382,15 +373,14 @@
             copy(i, p).wait()
 
 
-def events_kernel(events, gain, top, bottom, top_x, bottom_x, grad, pg):
-    for start, rows, mine, other in ((0, TOP, top, top_x), (TOP, BLOCK - TOP, bottom, bottom_x)):
-        x = events[start : start + rows, :].astype(F32)
-        inverse = lax.rsqrt(jnp.mean(x * x, axis=1, keepdims=True) + 1e-06)
-        gn = mine[:rows, :].astype(F32) + other[:rows, :].astype(F32)
-        scaled = gn * gain[...]
-        mean = jnp.mean(scaled * x, axis=1, keepdims=True)
-        grad[start : start + rows, :] = inverse * scaled - x * (inverse * inverse * inverse) * mean
-    pg[...] = join_rows(bottom[BLOCK - TOP :, :]) + join_rows(bottom_x[BLOCK - TOP :, :])
+def events_kernel(order, events, gain, mine, other, pg_a, pg_b, grad, pg):
+    x = events[...].astype(F32)
+    inverse = lax.rsqrt(jnp.mean(x * x, axis=1, keepdims=True) + 1e-06)
+    gn = mine[...].astype(F32) + other[...].astype(F32)
+    scaled = gn * gain[...]
+    mean = jnp.mean(scaled * x, axis=1, keepdims=True)
+    grad[...] = inverse * scaled - x * (inverse * inverse * inverse) * mean
+    pg[...] = pg_a[...] + pg_b[...]
 
 
 def output_kernel(where, mine, rep, mine_x, rep_x, ow, ow_x, out):
@@ -522,63 +512,58 @@
         sums = lax.psum(pack_q.astype(F32), "seq").astype(BF16)
         all_q = [sums[i] for i in range(CHUNKS)]
     (k_last,) = call(functools.partial(key_kernel, True), [acc_shape], [kv, qa_odd], [late], us=6)
-    oth_q = [swap(piece, "rep") for piece in all_q]
     last = after(where, k_last, mixed_x, all_q)
 
-    pack_kv, gn_own, gn_oth, _ = call(
-        key_finish_kernel,
-        [
-            shape((CHUNKS, 2 * step + GAIN_ROWS, w), BF16),
-            shape((BLOCK, D), BF16),
-            shape((BLOCK, D), BF16),
-            shape((rows2, 2 * w), BF16),
-        ],
-        [events, ev_oth, inv, slope_kv, normed_t, gp_gq, w4, k_own, k_far, k_last],
+    gn_own, gn_oth, gp_kv, share = call(
+        grad_normed_kernel,
+        [shape((BLOCK, D), BF16), shape((BLOCK, D), BF16), shape((rows2, 2 * w), BF16), shape((1, D), F32)],
+        [events, ev_oth, inv, slope_kv, gp_gq, w4, k_own, k_far, k_last],
         [last],
     )
-    late = where
-    if direct:
-        got_kv = scatter_over_seq(pack_kv)
-    halves = [shape((TOP, D), BF16), shape((BLOCK - TOP, D), BF16)]
-    top, bottom = call(add_cores_kernel, halves, [gn_own, swap(gn_oth, "rep")], [late])
+    (pack_kv,) = call(
+        key_weights_kernel, [shape((CHUNKS, 2 * step + GAIN_ROWS, w), BF16)], [normed_t, gp_kv, share]
+    )
+    got_kv = scatter_over_seq(pack_kv) if direct else []
+    (gn_blk,) = call(add_cores_kernel, [shape((BLOCK, D), BF16)], [gn_own, swap(gn_oth, "rep")], [where])
     if n_head == 2:
+        gn_x = swap(gn_blk, "head")
         (output,) = call(
             output_kernel,
             [shape((BLOCK, D), BF16)],
             [mix_own, mix_rep, *(mixed_x or [swap(mix_own, "head"), swap(mix_rep, "head")]), out_weight, ow_x],
             [where],
+            us=5,
         )
-        top_x = swap(top, "head")
     else:
         weight = jnp.where(rep == 0, out_weight, jnp.roll(out_weight, w, axis=0))
         mixed = jnp.concatenate([mix_own, mix_rep], axis=1)
         output = lax.psum(dot_nn(mixed, weight), "head").astype(BF16)
-        top, bottom = lax.psum((top.astype(F32), bottom.astype(F32)), "head")
-        top_x = jnp.zeros_like(top)
-    wide = shape((BLOCK - TOP + GAIN_ROWS, D), BF16)
+        gn_blk = lax.psum(gn_blk.astype(F32), "head")
+        gn_x = jnp.zeros_like(gn_blk)
+    cat_q = jnp.concatenate(all_q, axis=0)
+    grad_in, grad_out = assemble(where, [cat_q, swap(cat_q, "rep")], w)
     if direct:
-        sum_kv, bottom = call(
+        sum_kv, pg = call(
             add_chunks_gain_kernel,
-            [shape((2 * step, w), BF16), wide],
-            [*got_kv, bottom],
-            [after(where, output, oth_q)],
+            [shape((2 * step, w), BF16), shape((1, D), F32)],
+            got_kv,
+            [after(where, grad_out)],
         )
-        bottom_x = swap(bottom, "head")
+        pg_x = swap(pg, "head")
         all_kv = gather_over_seq(sum_kv)
     else:
         sums = lax.psum(pack_kv.astype(F32), "seq")
         all_kv = [sums[i, : 2 * step].astype(BF16) for i in range(CHUNKS)]
         pg = sums[0, 2 * step :]
-        pg = (pg[: D // w] + pg[D // w : 2 * (D // w)]).reshape(1, D)
-        pg = jnp.concatenate([pg, jnp.zeros((GAIN_ROWS - 1, D), F32)])
-        bottom, bottom_x = jnp.concatenate([bottom, lax.psum(pg, "head")]), jnp.zeros(wide.shape, F32)
+        pg = lax.psum((pg[: D // w] + pg[D // w : 2 * (D // w)]).reshape(1, D), "head")
+        pg_x = jnp.zeros_like(pg)
     grad_events, pg = call(
         events_kernel,
         [shape((BLOCK, D), F32), shape((1, D), F32)],
-        [events, gain, top, bottom, top_x, bottom_x],
-    )
-    grad_in, grad_out = assemble(late, [*all_q, *oth_q], w)
-    all_kv = after(all_kv, grad_out, pg)
+        [events, gain, gn_blk, gn_x, pg, pg_x],
+        [after(where, output)],
+    )
+    all_kv = after(all_kv, pg)
     oth_kv = [swap(piece, "rep") for piece in all_kv]
     grad_in, pg = assemble(where, [*all_kv, *oth_kv, pg, swap(pg, "rep")], w, grad_in)
     return (output, grad_events, grad_in, grad_out, pg.reshape(D))

time: 89.1 us -> 84.8 us (0.952)
  waiting for transfers between devices: 11.8 us -> 6.83 us
  Pallas kernels: 35.2 us -> 39.5 us
  starting transfers between devices: 40.6 us -> 37.3 us
    ppermute x31 -> x28, waiting for transfers between devices: 11.3 us -> 6.82 us  [swap(): return lax.ppermute(x, axis, [(i, i ^ bit) for i in range(n)])]
    pallas_call x14 -> x15, Pallas kernels: 30.6 us -> 34.9 us  [call(): pl.pallas_call(with_fetch if fetched else kernel, out_shape=out_shapes, i...]
    ppermute x31 -> x28, starting transfers between devices: 35.8 us -> 32.5 us  [swap(): return lax.ppermute(x, axis, [(i, i ^ bit) for i in range(n)])]
  transfers between devices with their start and end apart: 35 -> 32, of which waited for: 8 -> 4; matrix products, arithmetic and copies ran while one was open for 0% -> 1% of each run, Pallas kernels for 34% -> 41%
where the time goes in v1:
time: 84.8 us; the launch traced here: 85.3 us
  Pallas kernels  39.5 us (47%)
  starting transfers between devices  37.3 us (44%)
  waiting for transfers between devices  6.83 us (8%)
  between operations  1.15 us (1%)
    pallas_call x15, Pallas kernels, call(): pl.pallas_call(with_fetch if fetched else kernel, out_shape=out_shapes, i...  34.9 us
    ppermute x28, starting transfers between devices, swap(): return lax.ppermute(x, axis, [(i, i ^ bit) for i in range(n)])  32.5 us
    ppermute x28, waiting for transfers between devices, swap(): return lax.ppermute(x, axis, [(i, i ^ bit) for i in range(n)])  6.82 us
    pallas_call x2, Pallas kernels, assemble(): pl.pallas_call(functools.partial(assemble_kernel, 2 * len(held)), out_sha...  4.6 us
    ppermute x1, starting transfers between devices, body(): qa_even = lax.ppermute(qa, axes, even)  3.21 us
  transfers between devices with their start and end apart: 32, of which 4 were waited for; matrix products, arithmetic and copies ran while one was open for 1% of the time, Pallas kernels for 41%

profile of v1, /device:TPU:0, one launch (start us, length us, event | category | flops | bytes accessed | tf_op | source)
XLA Modules:
  0.0 85.3 jit_solution(8644777423221057396)
XLA Ops:
  1.7 2.6 %collective-permute-start.4 = (bf16[256,512]{1,0:T(8,128)(2,1)}, bf16[256,512]{1,0:T(8,128)(2,1)}, u32[]{:S(2)}, u32[]{:S(2)}) collective-permute-start(bf16[256,512]{1,0:T(8,128)(2,1)} %ow.1), channel_id=1, source_target_pairs={{0,2},{2,0},{1,3},{3,1},{4,6},{6,4},{5,7},{7,5},{8,10},{10,8},{9,1... | collective-permute-start | bytes 786440 | tf_op jit(solution)/shard_map/ppermute | solution.py:398
  4.7 2.2 %shard_map.101 = (bf16[1024,512]{1,0:T(8,128)(2,1)S(1)}, f32[1024,128]{1,0:T(8,128)S(1)}, f32[1024,256]{1,0:T(8,128)S(1)}, bf16[1024,256]{1,0:T(8,128)(2,1)S(1)}) custom-call(s32[8]{0:T(128)S(1)} %stack.39.refs_0_.where.order, bf16[512,512]{1,0:T(8,128)(2,1)S(1)} %copy-done.1, bf16[512,512]{1,0:T(8,128)(2,1)} %collective-permute-done.2.refs_2_.ev_oth, ...), custom_call_target="tpu_custom_call" | custom-call | tf_op jit(solution)/shard_map/pallas_call | solution.py:61
  6.9 1.6 %collective-permute-start.3 = (bf16[1024,256]{1,0:T(8,128)(2,1)S(1)}, bf16[1024,256]{1,0:T(8,128)(2,1)S(1)}, u32[]{:S(2)}, u32[]{:S(2)}) collective-permute-start(bf16[1024,256]{1,0:T(8,128)(2,1)S(1)} %get-tuple-element.46.kv), channel_id=1, source_target_pairs={{0,4},{1,5},{4,0},{5,1},{8,12},{9,13},{12,8},{13,9},{2,6},{3,7},{6... | collective-permute-start | bytes 1572872 | tf_op jit(solution)/shard_map/ppermute | solution.py:461
  8.6 1.8 %shard_map.102 = (f32[1024,256]{1,0:T(8,128)S(1)}, bf16[1040,256]{1,0:T(8,128)(2,1)S(1)}, bf16[1024,128]{1,0:T(8,128)(2,1)S(1)}, f32[1024,128]{1,0:T(8,128)S(1)}) custom-call(s32[8]{0:T(128)S(1)} %stack.39.refs_0_.where.order, s32[1,4]{1,0:T(1,128)S(1)} %copy-done.5, s32[1,4]{1,0:T(1,128)S(1)} %collective-permute-done.1.refs_2_.mask_oth, ...), custom_call_target="tpu_custom_call" | custom-call | tf_op jit(solution)/shard_map/pallas_call | solution.py:61
  10.3 3.2 %collective-permute-start.9 = (bf16[1040,256]{1,0:T(8,128)(2,1)S(1)}, bf16[1040,256]{1,0:T(8,128)(2,1)S(1)}, u32[]{:S(2)}, u32[]{:S(2)}) collective-permute-start(bf16[1040,256]{1,0:T(8,128)(2,1)S(1)} %get-tuple-element.45.qa), channel_id=1, source_target_pairs={{0,4},{1,5},{4,0},{5,1},{8,12},{9,13},{12,8},{13,9},{2,6},{3,7},{6... | collective-permute-start | bytes 1597448 | tf_op jit(solution)/shard_map/ppermute | solution.py:475
  13.6 9.8 %shard_map.103 = (f32[1024,256]{1,0:T(8,128)S(1)}, f32[1024,256]{1,0:T(8,128)S(1)}, bf16[512,1024]{1,0:T(8,128)(2,1)S(1)}) custom-call(s32[8]{0:T(128)S(1)} %stack.39.refs_0_.where.order, s32[1,4]{1,0:T(1,128)S(1)} %copy-done.5, s32[1,4]{1,0:T(1,128)S(1)} %collective-permute-done.1.refs_2_.mask_oth, bf16[1040,256]{1,0:T(8,128)(2,1)S(1)} %get-tuple-element.45.qa, ...), custom_call_target="tpu_custom_call" | custom-call | flops 9900000256 | tf_op jit(solution)/shard_map/pallas_call | solution.py:61
  23.3 3.6 %shard_map.104.acc_b = f32[1024,256]{1,0:T(8,128)S(1)} custom-call(s32[8]{0:T(128)S(1)} %stack.39.refs_0_.where.order, s32[1,4]{1,0:T(1,128)S(1)} %copy-done.5, s32[1,4]{1,0:T(1,128)S(1)} %collective-permute-done.1.refs_2_.mask_oth, bf16[1040,256]{1,0:T(8,128)(2,1)S(1)} %get-tuple-element.45.qa, bf16[1024,256]{1,0:T(8,128)(2,1)S(1)} %collective-permute-done.3.kv), custom_call_target="tpu_custom_call" | custom-call | flops 5500000256 | tf_op jit(solution)/shard_map/pallas_call | solution.py:61
  27.0 0.7 shard_map.105.acc_c
  27.7 1.5 %shard_map.106 = (bf16[512,128]{1,0:T(8,128)(2,1)S(1)}, bf16[512,128]{1,0:T(8,128)(2,1)S(1)}, bf16[1024,256]{1,0:T(8,128)(2,1)S(1)}, bf16[4,384,128]{2,1,0:T(8,128)(2,1)S(1)}) custom-call(s32[8]{0:T(128)S(1)} %stack.39.refs_0_.where.order, bf16[512,512]{1,0:T(8,128)(2,1)S(1)} %copy-done.2, bf16[512,512]{1,0:T(8,128)(2,1)S(1)} %collective-permute-done.refs_4_.cot_oth, ...), custom_call_target="tpu_custom_call" | custom-call | tf_op jit(solution)/shard_map/pallas_call | solution.py:61
  29.3 4.9 %collective-permute-start.10 = (bf16[384,128]{1,0:T(8,128)(2,1)S(1)}, bf16[384,128]{1,0:T(8,128)(2,1)S(1)}, u32[]{:S(2)}, u32[]{:S(2)}) collective-permute-start(bf16[384,128]{1,0:T(8,128)(2,1)S(1)} %get-tuple-element.79), channel_id=1, source_target_pairs={{0,4},{4,0},{8,12},{12,8},{1,5},{5,1},{9,13},{13,9},{2,6},{6,2},{1... | collective-permute-start | bytes 294920 | tf_op jit(solution)/shard_map/ppermute | solution.py:398
  34.2 2.4 %collective-permute-start.12 = (bf16[384,128]{1,0:T(8,128)(2,1)S(1)}, bf16[384,128]{1,0:T(8,128)(2,1)S(1)}, u32[]{:S(2)}, u32[]{:S(2)}) collective-permute-start(bf16[384,128]{1,0:T(8,128)(2,1)S(1)} %get-tuple-element.77), channel_id=1, source_target_pairs={{0,12},{4,8},{8,4},{12,0},{1,13},{5,9},{9,5},{13,1},{2,14},{6,10},... | collective-permute-start | bytes 294920 | tf_op jit(solution)/shard_map/ppermute | solution.py:398
  36.6 5.4 %shard_map.108.acc_b = f32[1024,256]{1,0:T(8,128)S(1)} custom-call(s32[8]{0:T(128)S(1)} %stack.39.refs_0_.where.order, bf16[1024,256]{1,0:T(8,128)(2,1)S(1)} %get-tuple-element.46.kv, bf16[1040,256]{1,0:T(8,128)(2,1)S(1)} %collective-permute-done.9.qa), custom_call_target="tpu_custom_call" | custom-call | flops 6600000000 | tf_op jit(solution)/shard_map/pallas_call | solution.py:61
  42.0 1.3 %collective-permute-start.7 = (bf16[512,128]{1,0:T(8,128)(2,1)S(1)}, bf16[512,128]{1,0:T(8,128)(2,1)S(1)}, u32[]{:S(2)}, u32[]{:S(2)}) collective-permute-start(bf16[512,128]{1,0:T(8,128)(2,1)S(1)} %get-tuple-element.50.mine), channel_id=1, source_target_pairs={{0,2},{2,0},{1,3},{3,1},{4,6},{6,4},{5,7},{7,5},{8,10},{10,8},{9,1... | collective-permute-start | bytes 393224 | tf_op jit(solution)/shard_map/ppermute | solution.py:398
  44.1 2.6 %collective-permute-start.14 = (bf16[384,128]{1,0:T(8,128)(2,1)S(1)}, bf16[384,128]{1,0:T(8,128)(2,1)S(1)}, u32[]{:S(2)}, u32[]{:S(2)}) collective-permute-start(bf16[384,128]{1,0:T(8,128)(2,1)S(1)} %shard_map.110), channel_id=1, source_target_pairs={{0,4},{4,0},{8,12},{12,8},{1,5},{5,1},{9,13},{13,9},{2,6},{6,2},{1... | collective-permute-start | bytes 294920 | tf_op jit(solution)/shard_map/ppermute | solution.py:398
  46.8 2.4 %collective-permute-start.16 = (bf16[384,128]{1,0:T(8,128)(2,1)S(1)}, bf16[384,128]{1,0:T(8,128)(2,1)S(1)}, u32[]{:S(2)}, u32[]{:S(2)}) collective-permute-start(bf16[384,128]{1,0:T(8,128)(2,1)S(1)} %shard_map.110), channel_id=1, source_target_pairs={{0,12},{4,8},{8,4},{12,0},{1,13},{5,9},{9,5},{13,1},{2,14},{6,10},... | collective-permute-start | bytes 294920 | tf_op jit(solution)/shard_map/ppermute | solution.py:398
  49.2 1.3 %collective-permute-start.8 = (bf16[512,128]{1,0:T(8,128)(2,1)S(1)}, bf16[512,128]{1,0:T(8,128)(2,1)S(1)}, u32[]{:S(2)}, u32[]{:S(2)}) collective-permute-start(bf16[512,128]{1,0:T(8,128)(2,1)S(1)} %collective-permute-done.6.rep), channel_id=1, source_target_pairs={{0,2},{2,0},{1,3},{3,1},{4,6},{6,4},{5,7},{7,5},{8,10},{10,8},{9,1... | collective-permute-start | bytes 393224 | tf_op jit(solution)/shard_map/ppermute | solution.py:398
  50.5 1.2 %shard_map.109.acc_c = f32[1024,256]{1,0:T(8,128)S(1)} custom-call(s32[8]{0:T(128)S(1)} %stack.39.refs_0_.where.order, bf16[1024,256]{1,0:T(8,128)(2,1)S(1)} %get-tuple-element.46.kv, bf16[1040,256]{1,0:T(8,128)(2,1)S(1)} %collective-permute-done.13.qa), custom_call_target="tpu_custom_call" | custom-call | flops 6600000000 | tf_op jit(solution)/shard_map/pallas_call | solution.py:61
  51.7 4.6 %collective-permute-done.15 = bf16[384,128]{1,0:T(8,128)(2,1)S(1)} collective-permute-done((bf16[384,128]{1,0:T(8,128)(2,1)S(1)}, bf16[384,128]{1,0:T(8,128)(2,1)S(1)}, u32[]{:S(2)}, u32[]{:S(2)}) %collective-permute-start.15) | collective-permute-done | bytes 98336 | tf_op jit(solution)/shard_map/ppermute | solution.py:398
  56.4 2.0 %shard_map.111 = (bf16[512,512]{1,0:T(8,128)(2,1)S(1)}, bf16[512,512]{1,0:T(8,128)(2,1)S(1)}, bf16[1024,256]{1,0:T(8,128)(2,1)S(1)}, f32[1,512]{1,0:T(1,128)S(1)}) custom-call(s32[8]{0:T(128)S(1)} %stack.39.refs_0_.where.order, bf16[512,512]{1,0:T(8,128)(2,1)S(1)} %copy-done.1, bf16[512,512]{1,0:T(8,128)(2,1)} %collective-permute-done.2.refs_2_.ev_oth, ...), custom_call_target="tpu_custom_call" | custom-call | tf_op jit(solution)/shard_map/pallas_call | solution.py:61
  59.5 2.6 %collective-permute-start.20 = (bf16[272,128]{1,0:T(8,128)(2,1)S(1)}, bf16[272,128]{1,0:T(8,128)(2,1)S(1)}, u32[]{:S(2)}, u32[]{:S(2)}) collective-permute-start(bf16[272,128]{1,0:T(8,128)(2,1)S(1)} %get-tuple-element.83), channel_id=1, source_target_pairs={{0,4},{4,0},{8,12},{12,8},{1,5},{5,1},{9,13},{13,9},{2,6},{6,2},{1... | collective-permute-start | bytes 208904 | tf_op jit(solution)/shard_map/ppermute | solution.py:398
  62.2 2.4 %collective-permute-start.22 = (bf16[272,128]{1,0:T(8,128)(2,1)S(1)}, bf16[272,128]{1,0:T(8,128)(2,1)S(1)}, u32[]{:S(2)}, u32[]{:S(2)}) collective-permute-start(bf16[272,128]{1,0:T(8,128)(2,1)S(1)} %get-tuple-element.81), channel_id=1, source_target_pairs={{0,12},{4,8},{8,4},{12,0},{1,13},{5,9},{9,5},{13,1},{2,14},{6,10},... | collective-permute-start | bytes 208904 | tf_op jit(solution)/shard_map/ppermute | solution.py:398
  64.6 0.7 shard_map.112.mine
  65.3 1.3 %collective-permute-start.18 = (bf16[512,512]{1,0:T(8,128)(2,1)S(1)}, bf16[512,512]{1,0:T(8,128)(2,1)S(1)}, u32[]{:S(2)}, u32[]{:S(2)}) collective-permute-start(bf16[512,512]{1,0:T(8,128)(2,1)S(1)} %shard_map.112.mine), channel_id=1, source_target_pairs={{0,2},{2,0},{1,3},{3,1},{4,6},{6,4},{5,7},{7,5},{8,10},{10,8},{9,1... | collective-permute-start | bytes 1572872 | tf_op jit(solution)/shard_map/ppermute | solution.py:398
  66.6 2.4 %shard_map.113 = (f32[512,4,256]{2,1,0:T(4,128)}, f32[256,512]{1,0:T(8,128)}) custom-call(s32[8]{0:T(128)S(1)} %stack.39.refs_0_.where.order, bf16[1536,128]{1,0:T(8,128)(2,1)S(1)} %pad_maximum_fusion.refs_0_, bf16[1536,128]{1,0:T(8,128)(2,1)S(1)} %collective-permute-done.19.refs_1_), custom_call_target="tpu_custom_call" | custom-call | tf_op jit(solution)/shard_map/pallas_call | solution.py:575
  69.0 0.8 collective-permute-done.21.refs_2_
  70.5 2.0 %collective-permute-start.24 = (bf16[256,128]{1,0:T(8,128)(2,1)S(1)}, bf16[256,128]{1,0:T(8,128)(2,1)S(1)}, u32[]{:S(2)}, u32[]{:S(2)}) collective-permute-start(bf16[256,128]{1,0:T(8,128)(2,1)S(1)} %get-tuple-element.70.refs_0_), channel_id=1, source_target_pairs={{0,4},{4,0},{8,12},{12,8},{1,5},{5,1},{9,13},{13,9},{2,6},{6,2},{1... | collective-permute-start | bytes 196616 | tf_op jit(solution)/shard_map/ppermute | solution.py:398
  72.7 2.2 %collective-permute-start.26 = (bf16[256,128]{1,0:T(8,128)(2,1)S(1)}, bf16[256,128]{1,0:T(8,128)(2,1)S(1)}, u32[]{:S(2)}, u32[]{:S(2)}) collective-permute-start(bf16[256,128]{1,0:T(8,128)(2,1)S(1)} %get-tuple-element.70.refs_0_), channel_id=1, source_target_pairs={{0,12},{4,8},{8,4},{12,0},{1,13},{5,9},{9,5},{13,1},{2,14},{6,10},... | collective-permute-start | bytes 196616 | tf_op jit(solution)/shard_map/ppermute | solution.py:398
  74.9 1.3 %collective-permute-start.23 = (f32[1,512]{1,0:T(1,128)S(1)}, f32[1,512]{1,0:T(1,128)S(1)}, u32[]{:S(2)}, u32[]{:S(2)}) collective-permute-start(f32[1,512]{1,0:T(1,128)S(1)} %get-tuple-element.66.pg_a), channel_id=1, source_target_pairs={{0,2},{2,0},{1,3},{3,1},{4,6},{6,4},{5,7},{7,5},{8,10},{10,8},{9,1... | collective-permute-start | bytes 6152 | tf_op jit(solution)/shard_map/ppermute | solution.py:398
  76.2 2.4 %shard_map.107 = bf16[512,512]{1,0:T(8,128)(2,1)} custom-call(s32[8]{0:T(128)S(1)} %stack.39.refs_0_.where.order, bf16[512,128]{1,0:T(8,128)(2,1)S(1)} %get-tuple-element.50.mine, bf16[512,128]{1,0:T(8,128)(2,1)S(1)} %collective-permute-done.6.rep, bf16[512,128]{1,0:T(8,128)(2,1)S(1)} %collective-permute-done.7.mine_x, ...), custom_call_target="tpu_custom_call" | custom-call | flops 5500000256 | tf_op jit(solution)/shard_map/pallas_call | solution.py:61
  78.7 2.0 %shard_map.116 = (f32[512,512]{1,0:T(8,128)}, f32[1,512]{1,0:T(1,128)S(1)}) custom-call(s32[8]{0:T(128)S(1)} %stack.39.refs_0_.where.order, bf16[512,512]{1,0:T(8,128)(2,1)S(1)} %copy-done.1, f32[1,512]{1,0:T(1,128)S(1)} %bitcast.33, bf16[512,512]{1,0:T(8,128)(2,1)S(1)} %shard_map.112.mine, bf16[512,512]{1,0:T(8,128)(2,1)S(1)} %collective-permute-done.18.other, ...), custom_call_target="tpu_custom_call" | custom-call | tf_op jit(solution)/shard_map/pallas_call | solution.py:61
  81.9 1.1 %collective-permute-done.31.refs_9_ = f32[1,512]{1,0:T(1,128)S(1)} collective-permute-done((f32[1,512]{1,0:T(1,128)S(1)}, f32[1,512]{1,0:T(1,128)S(1)}, u32[]{:S(2)}, u32[]{:S(2)}) %collective-permute-start.31) | collective-permute-done | bytes 2080 | tf_op jit(solution)/shard_map/ppermute | solution.py:398
  83.0 2.2 %shard_map.117 = (f32[512,4,256]{2,1,0:T(4,128)}, f32[1,512]{1,0:T(1,128)}) custom-call(s32[8]{0:T(128)S(1)} %stack.39.refs_0_.where.order, bf16[256,128]{1,0:T(8,128)(2,1)S(1)} %get-tuple-element.70.refs_0_, bf16[256,128]{1,0:T(8,128)(2,1)S(1)} %collective-permute-done.24.refs_1_, ...), custom_call_target="tpu_custom_call", output_to_operand_aliasing={{0}: (11, {})} | custom-call | tf_op jit(solution)/shard_map/pallas_call | solution.py:575
  (67 shorter events, 5.5 us)
Async XLA Ops:
  0.7 4.0 %collective-permute-start.2 = (bf16[512,512]{1,0:T(8,128)(2,1)}, bf16[512,512]{1,0:T(8,128)(2,1)}, u32[]{:S(2)}, u32[]{:S(2)}) collective-permute-start(bf16[512,512]{1,0:T(8,128)(2,1)} %events.1), channel_id=1, source_target_pairs={{0,1},{1,0},{2,3},{3,2},{4,5},{5,4},{6,7},{7,6},{8,9},{9,8},{10,11... | collective-permute-start | bytes 1572872 | tf_op jit(solution)/shard_map/ppermute | solution.py:398
  1.2 7.3 %collective-permute-start = (bf16[512,512]{1,0:T(8,128)(2,1)}, bf16[512,512]{1,0:T(8,128)(2,1)S(1)}, u32[]{:S(2)}, u32[]{:S(2)}) collective-permute-start(bf16[512,512]{1,0:T(8,128)(2,1)} %cot_own.1), channel_id=1, source_target_pairs={{0,1},{1,0},{2,3},{3,2},{4,5},{5,4},{6,7},{7,6},{8,9},{9,8},{10,11... | collective-permute-start | bytes 1572872 | tf_op jit(solution)/shard_map/ppermute | solution.py:398
  1.3 7.2 %collective-permute-start.1 = (s32[1,4]{1,0:T(1,128)}, s32[1,4]{1,0:T(1,128)S(1)}, u32[]{:S(2)}, u32[]{:S(2)}) collective-permute-start(s32[1,4]{1,0:T(1,128)} %mask_own.5), channel_id=1, source_target_pairs={{0,1},{1,0},{2,3},{3,2},{4,5},{5,4},{6,7},{7,6},{8,9},{9,8},{10,11... | collective-permute-start | bytes 56 | tf_op jit(solution)/shard_map/ppermute | solution.py:398
  1.7 25.2 %collective-permute-start.4 = (bf16[256,512]{1,0:T(8,128)(2,1)}, bf16[256,512]{1,0:T(8,128)(2,1)}, u32[]{:S(2)}, u32[]{:S(2)}) collective-permute-start(bf16[256,512]{1,0:T(8,128)(2,1)} %ow.1), channel_id=1, source_target_pairs={{0,2},{2,0},{1,3},{3,1},{4,6},{6,4},{5,7},{7,5},{8,10},{10,8},{9,1... | collective-permute-start | bytes 786440 | tf_op jit(solution)/shard_map/ppermute | solution.py:398
  6.9 16.4 %collective-permute-start.3 = (bf16[1024,256]{1,0:T(8,128)(2,1)S(1)}, bf16[1024,256]{1,0:T(8,128)(2,1)S(1)}, u32[]{:S(2)}, u32[]{:S(2)}) collective-permute-start(bf16[1024,256]{1,0:T(8,128)(2,1)S(1)} %get-tuple-element.46.kv), channel_id=1, source_target_pairs={{0,4},{1,5},{4,0},{5,1},{8,12},{9,13},{12,8},{13,9},{2,6},{3,7},{6... | collective-permute-start | bytes 1572872 | tf_op jit(solution)/shard_map/ppermute | solution.py:461
  8.5 18.4 %collective-permute-start.5 = (bf16[1024,256]{1,0:T(8,128)(2,1)S(1)}, bf16[1024,256]{1,0:T(8,128)(2,1)S(1)}, u32[]{:S(2)}, u32[]{:S(2)}) collective-permute-start(bf16[1024,256]{1,0:T(8,128)(2,1)S(1)} %get-tuple-element.46.kv), channel_id=1, source_target_pairs={{0,1},{1,0},{4,8},{5,9},{8,4},{9,5},{12,13},{13,12},{2,3},{3,2},{6... | collective-permute-start | bytes 1572872 | tf_op jit(solution)/shard_map/ppermute | solution.py:462
  10.3 26.3 %collective-permute-start.9 = (bf16[1040,256]{1,0:T(8,128)(2,1)S(1)}, bf16[1040,256]{1,0:T(8,128)(2,1)S(1)}, u32[]{:S(2)}, u32[]{:S(2)}) collective-permute-start(bf16[1040,256]{1,0:T(8,128)(2,1)S(1)} %get-tuple-element.45.qa), channel_id=1, source_target_pairs={{0,4},{1,5},{4,0},{5,1},{8,12},{9,13},{12,8},{13,9},{2,6},{3,7},{6... | collective-permute-start | bytes 1597448 | tf_op jit(solution)/shard_map/ppermute | solution.py:475
  13.6 33.2 %collective-permute-start.13 = (bf16[1040,256]{1,0:T(8,128)(2,1)S(1)}, bf16[1040,256]{1,0:T(8,128)(2,1)S(1)}, u32[]{:S(2)}, u32[]{:S(2)}) collective-permute-start(bf16[1040,256]{1,0:T(8,128)(2,1)S(1)} %get-tuple-element.45.qa), channel_id=1, source_target_pairs={{0,1},{1,0},{4,8},{5,9},{8,4},{9,5},{12,13},{13,12},{2,3},{3,2},{6... | collective-permute-start | bytes 1597448 | tf_op jit(solution)/shard_map/ppermute | solution.py:476
  29.3 12.8 %collective-permute-start.10 = (bf16[384,128]{1,0:T(8,128)(2,1)S(1)}, bf16[384,128]{1,0:T(8,128)(2,1)S(1)}, u32[]{:S(2)}, u32[]{:S(2)}) collective-permute-start(bf16[384,128]{1,0:T(8,128)(2,1)S(1)} %get-tuple-element.79), channel_id=1, source_target_pairs={{0,4},{4,0},{8,12},{12,8},{1,5},{5,1},{9,13},{13,9},{2,6},{6,2},{1... | collective-permute-start | bytes 294920 | tf_op jit(solution)/shard_map/ppermute | solution.py:398
  34.2 9.4 %collective-permute-start.11 = (bf16[384,128]{1,0:T(8,128)(2,1)S(1)}, bf16[384,128]{1,0:T(8,128)(2,1)S(1)}, u32[]{:S(2)}, u32[]{:S(2)}) collective-permute-start(bf16[384,128]{1,0:T(8,128)(2,1)S(1)} %get-tuple-element.78), channel_id=1, source_target_pairs={{0,8},{4,12},{8,0},{12,4},{1,9},{5,13},{9,1},{13,5},{2,10},{6,14},... | collective-permute-start | bytes 294920 | tf_op jit(solution)/shard_map/ppermute | solution.py:398
  34.2 9.4 %collective-permute-start.12 = (bf16[384,128]{1,0:T(8,128)(2,1)S(1)}, bf16[384,128]{1,0:T(8,128)(2,1)S(1)}, u32[]{:S(2)}, u32[]{:S(2)}) collective-permute-start(bf16[384,128]{1,0:T(8,128)(2,1)S(1)} %get-tuple-element.77), channel_id=1, source_target_pairs={{0,12},{4,8},{8,4},{12,0},{1,13},{5,9},{9,5},{13,1},{2,14},{6,10},... | collective-permute-start | bytes 294920 | tf_op jit(solution)/shard_map/ppermute | solution.py:398
  36.6 12.6 %collective-permute-start.6 = (bf16[512,128]{1,0:T(8,128)(2,1)S(1)}, bf16[512,128]{1,0:T(8,128)(2,1)S(1)}, u32[]{:S(2)}, u32[]{:S(2)}) collective-permute-start(bf16[512,128]{1,0:T(8,128)(2,1)S(1)} %get-tuple-element.51), channel_id=1, source_target_pairs={{0,1},{1,0},{2,3},{3,2},{4,5},{5,4},{6,7},{7,6},{8,9},{9,8},{10,11... | collective-permute-start | bytes 393224 | tf_op jit(solution)/shard_map/ppermute | solution.py:398
  42.0 9.6 %collective-permute-start.7 = (bf16[512,128]{1,0:T(8,128)(2,1)S(1)}, bf16[512,128]{1,0:T(8,128)(2,1)S(1)}, u32[]{:S(2)}, u32[]{:S(2)}) collective-permute-start(bf16[512,128]{1,0:T(8,128)(2,1)S(1)} %get-tuple-element.50.mine), channel_id=1, source_target_pairs={{0,2},{2,0},{1,3},{3,1},{4,6},{6,4},{5,7},{7,5},{8,10},{10,8},{9,1... | collective-permute-start | bytes 393224 | tf_op jit(solution)/shard_map/ppermute | solution.py:398
  44.1 7.6 %collective-permute-start.14 = (bf16[384,128]{1,0:T(8,128)(2,1)S(1)}, bf16[384,128]{1,0:T(8,128)(2,1)S(1)}, u32[]{:S(2)}, u32[]{:S(2)}) collective-permute-start(bf16[384,128]{1,0:T(8,128)(2,1)S(1)} %shard_map.110), channel_id=1, source_target_pairs={{0,4},{4,0},{8,12},{12,8},{1,5},{5,1},{9,13},{13,9},{2,6},{6,2},{1... | collective-permute-start | bytes 294920 | tf_op jit(solution)/shard_map/ppermute | solution.py:398
  46.8 9.6 %collective-permute-start.15 = (bf16[384,128]{1,0:T(8,128)(2,1)S(1)}, bf16[384,128]{1,0:T(8,128)(2,1)S(1)}, u32[]{:S(2)}, u32[]{:S(2)}) collective-permute-start(bf16[384,128]{1,0:T(8,128)(2,1)S(1)} %shard_map.110), channel_id=1, source_target_pairs={{0,8},{4,12},{8,0},{12,4},{1,9},{5,13},{9,1},{13,5},{2,10},{6,14},... | collective-permute-start | bytes 294920 | tf_op jit(solution)/shard_map/ppermute | solution.py:398
  46.8 9.6 %collective-permute-start.16 = (bf16[384,128]{1,0:T(8,128)(2,1)S(1)}, bf16[384,128]{1,0:T(8,128)(2,1)S(1)}, u32[]{:S(2)}, u32[]{:S(2)}) collective-permute-start(bf16[384,128]{1,0:T(8,128)(2,1)S(1)} %shard_map.110), channel_id=1, source_target_pairs={{0,12},{4,8},{8,4},{12,0},{1,13},{5,9},{9,5},{13,1},{2,14},{6,10},... | collective-permute-start | bytes 294920 | tf_op jit(solution)/shard_map/ppermute | solution.py:398
  49.2 7.1 %collective-permute-start.8 = (bf16[512,128]{1,0:T(8,128)(2,1)S(1)}, bf16[512,128]{1,0:T(8,128)(2,1)S(1)}, u32[]{:S(2)}, u32[]{:S(2)}) collective-permute-start(bf16[512,128]{1,0:T(8,128)(2,1)S(1)} %collective-permute-done.6.rep), channel_id=1, source_target_pairs={{0,2},{2,0},{1,3},{3,1},{4,6},{6,4},{5,7},{7,5},{8,10},{10,8},{9,1... | collective-permute-start | bytes 393224 | tf_op jit(solution)/shard_map/ppermute | solution.py:398
  58.4 6.2 %collective-permute-start.17 = (bf16[512,512]{1,0:T(8,128)(2,1)S(1)}, bf16[512,512]{1,0:T(8,128)(2,1)S(1)}, u32[]{:S(2)}, u32[]{:S(2)}) collective-permute-start(bf16[512,512]{1,0:T(8,128)(2,1)S(1)} %get-tuple-element.61), channel_id=1, source_target_pairs={{0,1},{1,0},{2,3},{3,2},{4,5},{5,4},{6,7},{7,6},{8,9},{9,8},{10,11... | collective-permute-start | bytes 1572872 | tf_op jit(solution)/shard_map/ppermute | solution.py:398
  58.5 8.1 %collective-permute-start.19 = (bf16[1536,128]{1,0:T(8,128)(2,1)S(1)}, bf16[1536,128]{1,0:T(8,128)(2,1)S(1)}, u32[]{:S(2)}, u32[]{:S(2)}) collective-permute-start(bf16[1536,128]{1,0:T(8,128)(2,1)S(1)} %pad_maximum_fusion.refs_0_), channel_id=1, source_target_pairs={{0,1},{1,0},{2,3},{3,2},{4,5},{5,4},{6,7},{7,6},{8,9},{9,8},{10,11... | collective-permute-start | bytes 1179656 | tf_op jit(solution)/shard_map/ppermute | solution.py:398
  59.5 9.5 %collective-permute-start.20 = (bf16[272,128]{1,0:T(8,128)(2,1)S(1)}, bf16[272,128]{1,0:T(8,128)(2,1)S(1)}, u32[]{:S(2)}, u32[]{:S(2)}) collective-permute-start(bf16[272,128]{1,0:T(8,128)(2,1)S(1)} %get-tuple-element.83), channel_id=1, source_target_pairs={{0,4},{4,0},{8,12},{12,8},{1,5},{5,1},{9,13},{13,9},{2,6},{6,2},{1... | collective-permute-start | bytes 208904 | tf_op jit(solution)/shard_map/ppermute | solution.py:398
  62.2 7.7 %collective-permute-start.21 = (bf16[272,128]{1,0:T(8,128)(2,1)S(1)}, bf16[272,128]{1,0:T(8,128)(2,1)S(1)}, u32[]{:S(2)}, u32[]{:S(2)}) collective-permute-start(bf16[272,128]{1,0:T(8,128)(2,1)S(1)} %get-tuple-element.82), channel_id=1, source_target_pairs={{0,8},{4,12},{8,0},{12,4},{1,9},{5,13},{9,1},{13,5},{2,10},{6,14},... | collective-permute-start | bytes 208904 | tf_op jit(solution)/shard_map/ppermute | solution.py:398
  62.2 7.7 %collective-permute-start.22 = (bf16[272,128]{1,0:T(8,128)(2,1)S(1)}, bf16[272,128]{1,0:T(8,128)(2,1)S(1)}, u32[]{:S(2)}, u32[]{:S(2)}) collective-permute-start(bf16[272,128]{1,0:T(8,128)(2,1)S(1)} %get-tuple-element.81), channel_id=1, source_target_pairs={{0,12},{4,8},{8,4},{12,0},{1,13},{5,9},{9,5},{13,1},{2,14},{6,10},... | collective-permute-start | bytes 208904 | tf_op jit(solution)/shard_map/ppermute | solution.py:398
  65.3 13.4 %collective-permute-start.18 = (bf16[512,512]{1,0:T(8,128)(2,1)S(1)}, bf16[512,512]{1,0:T(8,128)(2,1)S(1)}, u32[]{:S(2)}, u32[]{:S(2)}) collective-permute-start(bf16[512,512]{1,0:T(8,128)(2,1)S(1)} %shard_map.112.mine), channel_id=1, source_target_pairs={{0,2},{2,0},{1,3},{3,1},{4,6},{6,4},{5,7},{7,5},{8,10},{10,8},{9,1... | collective-permute-start | bytes 1572872 | tf_op jit(solution)/shard_map/ppermute | solution.py:398
  70.5 10.2 %collective-permute-start.24 = (bf16[256,128]{1,0:T(8,128)(2,1)S(1)}, bf16[256,128]{1,0:T(8,128)(2,1)S(1)}, u32[]{:S(2)}, u32[]{:S(2)}) collective-permute-start(bf16[256,128]{1,0:T(8,128)(2,1)S(1)} %get-tuple-element.70.refs_0_), channel_id=1, source_target_pairs={{0,4},{4,0},{8,12},{12,8},{1,5},{5,1},{9,13},{13,9},{2,6},{6,2},{1... | collective-permute-start | bytes 196616 | tf_op jit(solution)/shard_map/ppermute | solution.py:398
  72.4 8.2 %collective-permute-start.25 = (bf16[256,128]{1,0:T(8,128)(2,1)S(1)}, bf16[256,128]{1,0:T(8,128)(2,1)S(1)}, u32[]{:S(2)}, u32[]{:S(2)}) collective-permute-start(bf16[256,128]{1,0:T(8,128)(2,1)S(1)} %get-tuple-element.70.refs_0_), channel_id=1, source_target_pairs={{0,8},{4,12},{8,0},{12,4},{1,9},{5,13},{9,1},{13,5},{2,10},{6,14},... | collective-permute-start | bytes 196616 | tf_op jit(solution)/shard_map/ppermute | solution.py:398
  72.7 7.9 %collective-permute-start.26 = (bf16[256,128]{1,0:T(8,128)(2,1)S(1)}, bf16[256,128]{1,0:T(8,128)(2,1)S(1)}, u32[]{:S(2)}, u32[]{:S(2)}) collective-permute-start(bf16[256,128]{1,0:T(8,128)(2,1)S(1)} %get-tuple-element.70.refs_0_), channel_id=1, source_target_pairs={{0,12},{4,8},{8,4},{12,0},{1,13},{5,9},{9,5},{13,1},{2,14},{6,10},... | collective-permute-start | bytes 196616 | tf_op jit(solution)/shard_map/ppermute | solution.py:398
  74.9 3.8 %collective-permute-start.23 = (f32[1,512]{1,0:T(1,128)S(1)}, f32[1,512]{1,0:T(1,128)S(1)}, u32[]{:S(2)}, u32[]{:S(2)}) collective-permute-start(f32[1,512]{1,0:T(1,128)S(1)} %get-tuple-element.66.pg_a), channel_id=1, source_target_pairs={{0,2},{2,0},{1,3},{3,1},{4,6},{6,4},{5,7},{7,5},{8,10},{10,8},{9,1... | collective-permute-start | bytes 6152 | tf_op jit(solution)/shard_map/ppermute | solution.py:398
  80.7 2.2 %collective-permute-start.27 = (bf16[256,128]{1,0:T(8,128)(2,1)S(1)}, bf16[256,128]{1,0:T(8,128)(2,1)S(1)}, u32[]{:S(2)}, u32[]{:S(2)}) collective-permute-start(bf16[256,128]{1,0:T(8,128)(2,1)S(1)} %get-tuple-element.70.refs_0_), channel_id=1, source_target_pairs={{0,1},{1,0},{2,3},{3,2},{4,5},{5,4},{6,7},{7,6},{8,9},{9,8},{10,11... | collective-permute-start | bytes 196616 | tf_op jit(solution)/shard_map/ppermute | solution.py:398
  80.8 2.2 %collective-permute-start.28 = (bf16[256,128]{1,0:T(8,128)(2,1)S(1)}, bf16[256,128]{1,0:T(8,128)(2,1)S(1)}, u32[]{:S(2)}, u32[]{:S(2)}) collective-permute-start(bf16[256,128]{1,0:T(8,128)(2,1)S(1)} %collective-permute-done.24.refs_1_), channel_id=1, source_target_pairs={{0,1},{1,0},{2,3},{3,2},{4,5},{5,4},{6,7},{7,6},{8,9},{9,8},{10,11... | collective-permute-start | bytes 196616 | tf_op jit(solution)/shard_map/ppermute | solution.py:398
  81.3 1.7 %collective-permute-start.29 = (bf16[256,128]{1,0:T(8,128)(2,1)S(1)}, bf16[256,128]{1,0:T(8,128)(2,1)S(1)}, u32[]{:S(2)}, u32[]{:S(2)}) collective-permute-start(bf16[256,128]{1,0:T(8,128)(2,1)S(1)} %collective-permute-done.25.refs_2_), channel_id=1, source_target_pairs={{0,1},{1,0},{2,3},{3,2},{4,5},{5,4},{6,7},{7,6},{8,9},{9,8},{10,11... | collective-permute-start | bytes 196616 | tf_op jit(solution)/shard_map/ppermute | solution.py:398
  81.3 1.6 %collective-permute-start.30 = (bf16[256,128]{1,0:T(8,128)(2,1)S(1)}, bf16[256,128]{1,0:T(8,128)(2,1)S(1)}, u32[]{:S(2)}, u32[]{:S(2)}) collective-permute-start(bf16[256,128]{1,0:T(8,128)(2,1)S(1)} %collective-permute-done.26.refs_3_), channel_id=1, source_target_pairs={{0,1},{1,0},{2,3},{3,2},{4,5},{5,4},{6,7},{7,6},{8,9},{9,8},{10,11... | collective-permute-start | bytes 196616 | tf_op jit(solution)/shard_map/ppermute | solution.py:398
  81.8 1.2 %collective-permute-start.31 = (f32[1,512]{1,0:T(1,128)S(1)}, f32[1,512]{1,0:T(1,128)S(1)}, u32[]{:S(2)}, u32[]{:S(2)}) collective-permute-start(f32[1,512]{1,0:T(1,128)S(1)} %get-tuple-element.69.refs_8_), channel_id=1, source_target_pairs={{0,1},{1,0},{2,3},{3,2},{4,5},{5,4},{6,7},{7,6},{8,9},{9,8},{10,11... | collective-permute-start | bytes 6152 | tf_op jit(solution)/shard_map/ppermute | solution.py:398
  (6 other events, 35.3 us)

commit v2 on v1

--- a/solution.py
+++ b/solution.py
@@ -151,11 +151,12 @@
         xh, yh = jnp.where(on, xr, zero), jnp.where(on, yr, zero)
         u = dot_nt(x, xh)
         g = dot_nt(y, yh)
-        a = 1.0 + jnp.tanh(u)
-        m = u * a
-        slope = a + m * (2.0 - a)
-        acc_y = acc_y + dot_nn(m.astype(BF16), yh)
-        acc_x = acc_x + dot_nn((g * slope).astype(BF16), xh)
+        t = jnp.tanh(u)
+        a = 1.0 + t
+        m = (u * a).astype(BF16)
+        slope = a.astype(BF16) + m * (1.0 - t).astype(BF16)
+        acc_y = acc_y + dot_nn(m, yh)
+        acc_x = acc_x + dot_nn(g.astype(BF16) * slope, xh)
     acc[rows, :w] = acc_x
     acc[rows, w:] = acc_y
 

time: 84.8 us -> 84.5 us (level)
  Pallas kernels: 39.5 us -> 33 us
  waiting for transfers between devices: 6.83 us -> 11 us
  starting transfers between devices: 37.3 us -> 40.2 us
    pallas_call x15, Pallas kernels: 34.9 us -> 28.4 us  [call(): pl.pallas_call(with_fetch if fetched else kernel, out_shape=out_shapes, i...]
    ppermute x28, starting transfers between devices: 32.5 us -> 35.4 us  [swap(): return lax.ppermute(x, axis, [(i, i ^ bit) for i in range(n)])]
    ppermute x1, waiting for transfers between devices: 0.01 us -> 2.74 us  [body(): kv_even = lax.ppermute(kv, axes, even)]
    ppermute x28, waiting for transfers between devices: 6.82 us -> 8.3 us  [swap(): return lax.ppermute(x, axis, [(i, i ^ bit) for i in range(n)])]
  transfers between devices with their start and end apart: 32 -> 32, of which waited for: 4 -> 5; matrix products, arithmetic and copies ran while one was open for 1% -> 1% of each run, Pallas kernels for 41% -> 33%
where the time goes in v2:
time: 84.5 us; the launch traced here: 85.8 us
  starting transfers between devices  40.2 us (48%)
  Pallas kernels  33 us (39%)
  waiting for transfers between devices  11 us (13%)
  between operations  1.14 us (1%)
    ppermute x28, starting transfers between devices, swap(): return lax.ppermute(x, axis, [(i, i ^ bit) for i in range(n)])  35.4 us
    pallas_call x15, Pallas kernels, call(): pl.pallas_call(with_fetch if fetched else kernel, out_shape=out_shapes, i...  28.4 us
    ppermute x28, waiting for transfers between devices, swap(): return lax.ppermute(x, axis, [(i, i ^ bit) for i in range(n)])  8.3 us
    pallas_call x2, Pallas kernels, assemble(): pl.pallas_call(functools.partial(assemble_kernel, 2 * len(held)), out_sha...  4.6 us
    ppermute x1, starting transfers between devices, body(): qa_even = lax.ppermute(qa, axes, even)  3.21 us
    ppermute x1, waiting for transfers between devices, body(): kv_even = lax.ppermute(kv, axes, even)  2.74 us
  transfers between devices with their start and end apart: 32, of which 5 were waited for; matrix products, arithmetic and copies ran while one was open for 1% of the time, Pallas kernels for 33%

profile of v2, /device:TPU:0, one launch (start us, length us, event | category | flops | bytes accessed | tf_op | source)
XLA Modules:
  0.0 85.8 jit_solution(17913199139621711004)
XLA Ops:
  1.7 2.6 %collective-permute-start.4 = (bf16[256,512]{1,0:T(8,128)(2,1)}, bf16[256,512]{1,0:T(8,128)(2,1)}, u32[]{:S(2)}, u32[]{:S(2)}) collective-permute-start(bf16[256,512]{1,0:T(8,128)(2,1)} %ow.1), channel_id=1, source_target_pairs={{0,2},{2,0},{1,3},{3,1},{4,6},{6,4},{5,7},{7,5},{8,10},{10,8},{9,1... | collective-permute-start | bytes 786440 | tf_op jit(solution)/shard_map/ppermute | solution.py:399
  4.7 2.2 %shard_map.101 = (bf16[1024,512]{1,0:T(8,128)(2,1)S(1)}, f32[1024,128]{1,0:T(8,128)S(1)}, f32[1024,256]{1,0:T(8,128)S(1)}, bf16[1024,256]{1,0:T(8,128)(2,1)S(1)}) custom-call(s32[8]{0:T(128)S(1)} %stack.39.refs_0_.where.order, bf16[512,512]{1,0:T(8,128)(2,1)S(1)} %copy-done.1, bf16[512,512]{1,0:T(8,128)(2,1)} %collective-permute-done.2.refs_2_.ev_oth, ...), custom_call_target="tpu_custom_call" | custom-call | tf_op jit(solution)/shard_map/pallas_call | solution.py:61
  6.9 1.6 %collective-permute-start.3 = (bf16[1024,256]{1,0:T(8,128)(2,1)S(1)}, bf16[1024,256]{1,0:T(8,128)(2,1)S(1)}, u32[]{:S(2)}, u32[]{:S(2)}) collective-permute-start(bf16[1024,256]{1,0:T(8,128)(2,1)S(1)} %get-tuple-element.46.kv), channel_id=1, source_target_pairs={{0,4},{1,5},{4,0},{5,1},{8,12},{9,13},{12,8},{13,9},{2,6},{3,7},{6... | collective-permute-start | bytes 1572872 | tf_op jit(solution)/shard_map/ppermute | solution.py:462
  8.6 1.8 %shard_map.102 = (f32[1024,256]{1,0:T(8,128)S(1)}, bf16[1040,256]{1,0:T(8,128)(2,1)S(1)}, bf16[1024,128]{1,0:T(8,128)(2,1)S(1)}, f32[1024,128]{1,0:T(8,128)S(1)}) custom-call(s32[8]{0:T(128)S(1)} %stack.39.refs_0_.where.order, s32[1,4]{1,0:T(1,128)S(1)} %copy-done.5, s32[1,4]{1,0:T(1,128)S(1)} %collective-permute-done.1.refs_2_.mask_oth, ...), custom_call_target="tpu_custom_call" | custom-call | tf_op jit(solution)/shard_map/pallas_call | solution.py:61
  10.3 3.2 %collective-permute-start.9 = (bf16[1040,256]{1,0:T(8,128)(2,1)S(1)}, bf16[1040,256]{1,0:T(8,128)(2,1)S(1)}, u32[]{:S(2)}, u32[]{:S(2)}) collective-permute-start(bf16[1040,256]{1,0:T(8,128)(2,1)S(1)} %get-tuple-element.45.qa), channel_id=1, source_target_pairs={{0,4},{1,5},{4,0},{5,1},{8,12},{9,13},{12,8},{13,9},{2,6},{3,7},{6... | collective-permute-start | bytes 1597448 | tf_op jit(solution)/shard_map/ppermute | solution.py:476
  13.6 5.4 %shard_map.103 = (f32[1024,256]{1,0:T(8,128)S(1)}, f32[1024,256]{1,0:T(8,128)S(1)}, bf16[512,1024]{1,0:T(8,128)(2,1)S(1)}) custom-call(s32[8]{0:T(128)S(1)} %stack.39.refs_0_.where.order, s32[1,4]{1,0:T(1,128)S(1)} %copy-done.5, s32[1,4]{1,0:T(1,128)S(1)} %collective-permute-done.1.refs_2_.mask_oth, bf16[1040,256]{1,0:T(8,128)(2,1)S(1)} %get-tuple-element.45.qa, ...), custom_call_target="tpu_custom_call" | custom-call | flops 9900000256 | tf_op jit(solution)/shard_map/pallas_call | solution.py:61
  19.0 2.7 %collective-permute-done.3.kv = bf16[1024,256]{1,0:T(8,128)(2,1)S(1)} collective-permute-done((bf16[1024,256]{1,0:T(8,128)(2,1)S(1)}, bf16[1024,256]{1,0:T(8,128)(2,1)S(1)}, u32[]{:S(2)}, u32[]{:S(2)}) %collective-permute-start.3) | collective-permute-done | bytes 524320 | tf_op jit(solution)/shard_map/ppermute | solution.py:462
  21.7 2.0 %shard_map.104.acc_b = f32[1024,256]{1,0:T(8,128)S(1)} custom-call(s32[8]{0:T(128)S(1)} %stack.39.refs_0_.where.order, s32[1,4]{1,0:T(1,128)S(1)} %copy-done.5, s32[1,4]{1,0:T(1,128)S(1)} %collective-permute-done.1.refs_2_.mask_oth, bf16[1040,256]{1,0:T(8,128)(2,1)S(1)} %get-tuple-element.45.qa, bf16[1024,256]{1,0:T(8,128)(2,1)S(1)} %collective-permute-done.3.kv), custom_call_target="tpu_custom_call" | custom-call | flops 5500000256 | tf_op jit(solution)/shard_map/pallas_call | solution.py:61
  24.4 1.5 %shard_map.106 = (bf16[512,128]{1,0:T(8,128)(2,1)S(1)}, bf16[512,128]{1,0:T(8,128)(2,1)S(1)}, bf16[1024,256]{1,0:T(8,128)(2,1)S(1)}, bf16[4,384,128]{2,1,0:T(8,128)(2,1)S(1)}) custom-call(s32[8]{0:T(128)S(1)} %stack.39.refs_0_.where.order, bf16[512,512]{1,0:T(8,128)(2,1)S(1)} %copy-done.2, bf16[512,512]{1,0:T(8,128)(2,1)S(1)} %collective-permute-done.refs_4_.cot_oth, ...), custom_call_target="tpu_custom_call" | custom-call | tf_op jit(solution)/shard_map/pallas_call | solution.py:61
  26.0 8.6 %collective-permute-start.10 = (bf16[384,128]{1,0:T(8,128)(2,1)S(1)}, bf16[384,128]{1,0:T(8,128)(2,1)S(1)}, u32[]{:S(2)}, u32[]{:S(2)}) collective-permute-start(bf16[384,128]{1,0:T(8,128)(2,1)S(1)} %get-tuple-element.79), channel_id=1, source_target_pairs={{0,4},{4,0},{8,12},{12,8},{1,5},{5,1},{9,13},{13,9},{2,6},{6,2},{1... | collective-permute-start | bytes 294920 | tf_op jit(solution)/shard_map/ppermute | solution.py:399
  34.6 1.1 %collective-permute-start.11 = (bf16[384,128]{1,0:T(8,128)(2,1)S(1)}, bf16[384,128]{1,0:T(8,128)(2,1)S(1)}, u32[]{:S(2)}, u32[]{:S(2)}) collective-permute-start(bf16[384,128]{1,0:T(8,128)(2,1)S(1)} %get-tuple-element.78), channel_id=1, source_target_pairs={{0,8},{4,12},{8,0},{12,4},{1,9},{5,13},{9,1},{13,5},{2,10},{6,14},... | collective-permute-start | bytes 294920 | tf_op jit(solution)/shard_map/ppermute | solution.py:399
  35.7 1.4 %collective-permute-start.12 = (bf16[384,128]{1,0:T(8,128)(2,1)S(1)}, bf16[384,128]{1,0:T(8,128)(2,1)S(1)}, u32[]{:S(2)}, u32[]{:S(2)}) collective-permute-start(bf16[384,128]{1,0:T(8,128)(2,1)S(1)} %get-tuple-element.77), channel_id=1, source_target_pairs={{0,12},{4,8},{8,4},{12,0},{1,13},{5,9},{9,5},{13,1},{2,14},{6,10},... | collective-permute-start | bytes 294920 | tf_op jit(solution)/shard_map/ppermute | solution.py:399
  37.1 4.9 %shard_map.108.acc_b = f32[1024,256]{1,0:T(8,128)S(1)} custom-call(s32[8]{0:T(128)S(1)} %stack.39.refs_0_.where.order, bf16[1024,256]{1,0:T(8,128)(2,1)S(1)} %get-tuple-element.46.kv, bf16[1040,256]{1,0:T(8,128)(2,1)S(1)} %collective-permute-done.9.qa), custom_call_target="tpu_custom_call" | custom-call | flops 6600000000 | tf_op jit(solution)/shard_map/pallas_call | solution.py:61
  42.0 1.3 %collective-permute-start.7 = (bf16[512,128]{1,0:T(8,128)(2,1)S(1)}, bf16[512,128]{1,0:T(8,128)(2,1)S(1)}, u32[]{:S(2)}, u32[]{:S(2)}) collective-permute-start(bf16[512,128]{1,0:T(8,128)(2,1)S(1)} %get-tuple-element.50.mine), channel_id=1, source_target_pairs={{0,2},{2,0},{1,3},{3,1},{4,6},{6,4},{5,7},{7,5},{8,10},{10,8},{9,1... | collective-permute-start | bytes 393224 | tf_op jit(solution)/shard_map/ppermute | solution.py:399
  43.3 1.3 %collective-permute-done.11.c = bf16[384,128]{1,0:T(8,128)(2,1)S(1)} collective-permute-done((bf16[384,128]{1,0:T(8,128)(2,1)S(1)}, bf16[384,128]{1,0:T(8,128)(2,1)S(1)}, u32[]{:S(2)}, u32[]{:S(2)}) %collective-permute-start.11) | collective-permute-done | bytes 98336 | tf_op jit(solution)/shard_map/ppermute | solution.py:399
  45.2 2.2 %collective-permute-start.14 = (bf16[384,128]{1,0:T(8,128)(2,1)S(1)}, bf16[384,128]{1,0:T(8,128)(2,1)S(1)}, u32[]{:S(2)}, u32[]{:S(2)}) collective-permute-start(bf16[384,128]{1,0:T(8,128)(2,1)S(1)} %shard_map.110), channel_id=1, source_target_pairs={{0,4},{4,0},{8,12},{12,8},{1,5},{5,1},{9,13},{13,9},{2,6},{6,2},{1... | collective-permute-start | bytes 294920 | tf_op jit(solution)/shard_map/ppermute | solution.py:399
  48.2 1.5 %collective-permute-start.16 = (bf16[384,128]{1,0:T(8,128)(2,1)S(1)}, bf16[384,128]{1,0:T(8,128)(2,1)S(1)}, u32[]{:S(2)}, u32[]{:S(2)}) collective-permute-start(bf16[384,128]{1,0:T(8,128)(2,1)S(1)} %shard_map.110), channel_id=1, source_target_pairs={{0,12},{4,8},{8,4},{12,0},{1,13},{5,9},{9,5},{13,1},{2,14},{6,10},... | collective-permute-start | bytes 294920 | tf_op jit(solution)/shard_map/ppermute | solution.py:399
  49.8 1.3 %collective-permute-start.8 = (bf16[512,128]{1,0:T(8,128)(2,1)S(1)}, bf16[512,128]{1,0:T(8,128)(2,1)S(1)}, u32[]{:S(2)}, u32[]{:S(2)}) collective-permute-start(bf16[512,128]{1,0:T(8,128)(2,1)S(1)} %collective-permute-done.6.rep), channel_id=1, source_target_pairs={{0,2},{2,0},{1,3},{3,1},{4,6},{6,4},{5,7},{7,5},{8,10},{10,8},{9,1... | collective-permute-start | bytes 393224 | tf_op jit(solution)/shard_map/ppermute | solution.py:399
  51.1 1.2 %shard_map.109.acc_c = f32[1024,256]{1,0:T(8,128)S(1)} custom-call(s32[8]{0:T(128)S(1)} %stack.39.refs_0_.where.order, bf16[1024,256]{1,0:T(8,128)(2,1)S(1)} %get-tuple-element.46.kv, bf16[1040,256]{1,0:T(8,128)(2,1)S(1)} %collective-permute-done.13.qa), custom_call_target="tpu_custom_call" | custom-call | flops 6600000000 | tf_op jit(solution)/shard_map/pallas_call | solution.py:61
  52.3 4.5 %collective-permute-done.15 = bf16[384,128]{1,0:T(8,128)(2,1)S(1)} collective-permute-done((bf16[384,128]{1,0:T(8,128)(2,1)S(1)}, bf16[384,128]{1,0:T(8,128)(2,1)S(1)}, u32[]{:S(2)}, u32[]{:S(2)}) %collective-permute-start.15) | collective-permute-done | bytes 98336 | tf_op jit(solution)/shard_map/ppermute | solution.py:399
  56.8 2.0 %shard_map.111 = (bf16[512,512]{1,0:T(8,128)(2,1)S(1)}, bf16[512,512]{1,0:T(8,128)(2,1)S(1)}, bf16[1024,256]{1,0:T(8,128)(2,1)S(1)}, f32[1,512]{1,0:T(1,128)S(1)}) custom-call(s32[8]{0:T(128)S(1)} %stack.39.refs_0_.where.order, bf16[512,512]{1,0:T(8,128)(2,1)S(1)} %copy-done.1, bf16[512,512]{1,0:T(8,128)(2,1)} %collective-permute-done.2.refs_2_.ev_oth, ...), custom_call_target="tpu_custom_call" | custom-call | tf_op jit(solution)/shard_map/pallas_call | solution.py:61
  60.0 2.2 %collective-permute-start.20 = (bf16[272,128]{1,0:T(8,128)(2,1)S(1)}, bf16[272,128]{1,0:T(8,128)(2,1)S(1)}, u32[]{:S(2)}, u32[]{:S(2)}) collective-permute-start(bf16[272,128]{1,0:T(8,128)(2,1)S(1)} %get-tuple-element.83), channel_id=1, source_target_pairs={{0,4},{4,0},{8,12},{12,8},{1,5},{5,1},{9,13},{13,9},{2,6},{6,2},{1... | collective-permute-start | bytes 208904 | tf_op jit(solution)/shard_map/ppermute | solution.py:399
  62.5 2.1 %collective-permute-start.22 = (bf16[272,128]{1,0:T(8,128)(2,1)S(1)}, bf16[272,128]{1,0:T(8,128)(2,1)S(1)}, u32[]{:S(2)}, u32[]{:S(2)}) collective-permute-start(bf16[272,128]{1,0:T(8,128)(2,1)S(1)} %get-tuple-element.81), channel_id=1, source_target_pairs={{0,12},{4,8},{8,4},{12,0},{1,13},{5,9},{9,5},{13,1},{2,14},{6,10},... | collective-permute-start | bytes 208904 | tf_op jit(solution)/shard_map/ppermute | solution.py:399
  65.3 1.3 %collective-permute-start.18 = (bf16[512,512]{1,0:T(8,128)(2,1)S(1)}, bf16[512,512]{1,0:T(8,128)(2,1)S(1)}, u32[]{:S(2)}, u32[]{:S(2)}) collective-permute-start(bf16[512,512]{1,0:T(8,128)(2,1)S(1)} %shard_map.112.mine), channel_id=1, source_target_pairs={{0,2},{2,0},{1,3},{3,1},{4,6},{6,4},{5,7},{7,5},{8,10},{10,8},{9,1... | collective-permute-start | bytes 1572872 | tf_op jit(solution)/shard_map/ppermute | solution.py:399
  66.6 2.4 %shard_map.113 = (f32[512,4,256]{2,1,0:T(4,128)}, f32[256,512]{1,0:T(8,128)}) custom-call(s32[8]{0:T(128)S(1)} %stack.39.refs_0_.where.order, bf16[1536,128]{1,0:T(8,128)(2,1)S(1)} %pad_maximum_fusion.refs_0_, bf16[1536,128]{1,0:T(8,128)(2,1)S(1)} %collective-permute-done.19.refs_1_), custom_call_target="tpu_custom_call" | custom-call | tf_op jit(solution)/shard_map/pallas_call | solution.py:576
  69.0 1.4 %collective-permute-done.21.refs_2_ = bf16[272,128]{1,0:T(8,128)(2,1)S(1)} collective-permute-done((bf16[272,128]{1,0:T(8,128)(2,1)S(1)}, bf16[272,128]{1,0:T(8,128)(2,1)S(1)}, u32[]{:S(2)}, u32[]{:S(2)}) %collective-permute-start.21) | collective-permute-done | bytes 69664 | tf_op jit(solution)/shard_map/ppermute | solution.py:399
  71.0 1.5 %collective-permute-start.24 = (bf16[256,128]{1,0:T(8,128)(2,1)S(1)}, bf16[256,128]{1,0:T(8,128)(2,1)S(1)}, u32[]{:S(2)}, u32[]{:S(2)}) collective-permute-start(bf16[256,128]{1,0:T(8,128)(2,1)S(1)} %get-tuple-element.70.refs_0_), channel_id=1, source_target_pairs={{0,4},{4,0},{8,12},{12,8},{1,5},{5,1},{9,13},{13,9},{2,6},{6,2},{1... | collective-permute-start | bytes 196616 | tf_op jit(solution)/shard_map/ppermute | solution.py:399
  73.2 2.2 %collective-permute-start.26 = (bf16[256,128]{1,0:T(8,128)(2,1)S(1)}, bf16[256,128]{1,0:T(8,128)(2,1)S(1)}, u32[]{:S(2)}, u32[]{:S(2)}) collective-permute-start(bf16[256,128]{1,0:T(8,128)(2,1)S(1)} %get-tuple-element.70.refs_0_), channel_id=1, source_target_pairs={{0,12},{4,8},{8,4},{12,0},{1,13},{5,9},{9,5},{13,1},{2,14},{6,10},... | collective-permute-start | bytes 196616 | tf_op jit(solution)/shard_map/ppermute | solution.py:399
  75.5 1.3 %collective-permute-start.23 = (f32[1,512]{1,0:T(1,128)S(1)}, f32[1,512]{1,0:T(1,128)S(1)}, u32[]{:S(2)}, u32[]{:S(2)}) collective-permute-start(f32[1,512]{1,0:T(1,128)S(1)} %get-tuple-element.66.pg_a), channel_id=1, source_target_pairs={{0,2},{2,0},{1,3},{3,1},{4,6},{6,4},{5,7},{7,5},{8,10},{10,8},{9,1... | collective-permute-start | bytes 6152 | tf_op jit(solution)/shard_map/ppermute | solution.py:399
  76.7 2.4 %shard_map.107 = bf16[512,512]{1,0:T(8,128)(2,1)} custom-call(s32[8]{0:T(128)S(1)} %stack.39.refs_0_.where.order, bf16[512,128]{1,0:T(8,128)(2,1)S(1)} %get-tuple-element.50.mine, bf16[512,128]{1,0:T(8,128)(2,1)S(1)} %collective-permute-done.6.rep, bf16[512,128]{1,0:T(8,128)(2,1)S(1)} %collective-permute-done.7.mine_x, ...), custom_call_target="tpu_custom_call" | custom-call | flops 5500000256 | tf_op jit(solution)/shard_map/pallas_call | solution.py:61
  79.2 2.0 %shard_map.116 = (f32[512,512]{1,0:T(8,128)}, f32[1,512]{1,0:T(1,128)S(1)}) custom-call(s32[8]{0:T(128)S(1)} %stack.39.refs_0_.where.order, bf16[512,512]{1,0:T(8,128)(2,1)S(1)} %copy-done.1, f32[1,512]{1,0:T(1,128)S(1)} %bitcast.33, bf16[512,512]{1,0:T(8,128)(2,1)S(1)} %shard_map.112.mine, bf16[512,512]{1,0:T(8,128)(2,1)S(1)} %collective-permute-done.18.other, ...), custom_call_target="tpu_custom_call" | custom-call | tf_op jit(solution)/shard_map/pallas_call | solution.py:61
  83.5 2.2 %shard_map.117 = (f32[512,4,256]{2,1,0:T(4,128)}, f32[1,512]{1,0:T(1,128)}) custom-call(s32[8]{0:T(128)S(1)} %stack.39.refs_0_.where.order, bf16[256,128]{1,0:T(8,128)(2,1)S(1)} %get-tuple-element.70.refs_0_, bf16[256,128]{1,0:T(8,128)(2,1)S(1)} %collective-permute-done.24.refs_1_, ...), custom_call_target="tpu_custom_call", output_to_operand_aliasing={{0}: (11, {})} | custom-call | tf_op jit(solution)/shard_map/pallas_call | solution.py:576
  (67 shorter events, 9.4 us)
Async XLA Ops:
  0.7 4.0 %collective-permute-start.2 = (bf16[512,512]{1,0:T(8,128)(2,1)}, bf16[512,512]{1,0:T(8,128)(2,1)}, u32[]{:S(2)}, u32[]{:S(2)}) collective-permute-start(bf16[512,512]{1,0:T(8,128)(2,1)} %events.1), channel_id=1, source_target_pairs={{0,1},{1,0},{2,3},{3,2},{4,5},{5,4},{6,7},{7,6},{8,9},{9,8},{10,11... | collective-permute-start | bytes 1572872 | tf_op jit(solution)/shard_map/ppermute | solution.py:399
  1.2 7.3 %collective-permute-start = (bf16[512,512]{1,0:T(8,128)(2,1)}, bf16[512,512]{1,0:T(8,128)(2,1)S(1)}, u32[]{:S(2)}, u32[]{:S(2)}) collective-permute-start(bf16[512,512]{1,0:T(8,128)(2,1)} %cot_own.1), channel_id=1, source_target_pairs={{0,1},{1,0},{2,3},{3,2},{4,5},{5,4},{6,7},{7,6},{8,9},{9,8},{10,11... | collective-permute-start | bytes 1572872 | tf_op jit(solution)/shard_map/ppermute | solution.py:399
  1.3 7.2 %collective-permute-start.1 = (s32[1,4]{1,0:T(1,128)}, s32[1,4]{1,0:T(1,128)S(1)}, u32[]{:S(2)}, u32[]{:S(2)}) collective-permute-start(s32[1,4]{1,0:T(1,128)} %mask_own.5), channel_id=1, source_target_pairs={{0,1},{1,0},{2,3},{3,2},{4,5},{5,4},{6,7},{7,6},{8,9},{9,8},{10,11... | collective-permute-start | bytes 56 | tf_op jit(solution)/shard_map/ppermute | solution.py:399
  1.7 22.0 %collective-permute-start.4 = (bf16[256,512]{1,0:T(8,128)(2,1)}, bf16[256,512]{1,0:T(8,128)(2,1)}, u32[]{:S(2)}, u32[]{:S(2)}) collective-permute-start(bf16[256,512]{1,0:T(8,128)(2,1)} %ow.1), channel_id=1, source_target_pairs={{0,2},{2,0},{1,3},{3,1},{4,6},{6,4},{5,7},{7,5},{8,10},{10,8},{9,1... | collective-permute-start | bytes 786440 | tf_op jit(solution)/shard_map/ppermute | solution.py:399
  6.9 14.8 %collective-permute-start.3 = (bf16[1024,256]{1,0:T(8,128)(2,1)S(1)}, bf16[1024,256]{1,0:T(8,128)(2,1)S(1)}, u32[]{:S(2)}, u32[]{:S(2)}) collective-permute-start(bf16[1024,256]{1,0:T(8,128)(2,1)S(1)} %get-tuple-element.46.kv), channel_id=1, source_target_pairs={{0,4},{1,5},{4,0},{5,1},{8,12},{9,13},{12,8},{13,9},{2,6},{3,7},{6... | collective-permute-start | bytes 1572872 | tf_op jit(solution)/shard_map/ppermute | solution.py:462
  8.5 15.2 %collective-permute-start.5 = (bf16[1024,256]{1,0:T(8,128)(2,1)S(1)}, bf16[1024,256]{1,0:T(8,128)(2,1)S(1)}, u32[]{:S(2)}, u32[]{:S(2)}) collective-permute-start(bf16[1024,256]{1,0:T(8,128)(2,1)S(1)} %get-tuple-element.46.kv), channel_id=1, source_target_pairs={{0,1},{1,0},{4,8},{5,9},{8,4},{9,5},{12,13},{13,12},{2,3},{3,2},{6... | collective-permute-start | bytes 1572872 | tf_op jit(solution)/shard_map/ppermute | solution.py:463
  10.3 26.7 %collective-permute-start.9 = (bf16[1040,256]{1,0:T(8,128)(2,1)S(1)}, bf16[1040,256]{1,0:T(8,128)(2,1)S(1)}, u32[]{:S(2)}, u32[]{:S(2)}) collective-permute-start(bf16[1040,256]{1,0:T(8,128)(2,1)S(1)} %get-tuple-element.45.qa), channel_id=1, source_target_pairs={{0,4},{1,5},{4,0},{5,1},{8,12},{9,13},{12,8},{13,9},{2,6},{3,7},{6... | collective-permute-start | bytes 1597448 | tf_op jit(solution)/shard_map/ppermute | solution.py:476
  13.6 34.7 %collective-permute-start.13 = (bf16[1040,256]{1,0:T(8,128)(2,1)S(1)}, bf16[1040,256]{1,0:T(8,128)(2,1)S(1)}, u32[]{:S(2)}, u32[]{:S(2)}) collective-permute-start(bf16[1040,256]{1,0:T(8,128)(2,1)S(1)} %get-tuple-element.45.qa), channel_id=1, source_target_pairs={{0,1},{1,0},{4,8},{5,9},{8,4},{9,5},{12,13},{13,12},{2,3},{3,2},{6... | collective-permute-start | bytes 1597448 | tf_op jit(solution)/shard_map/ppermute | solution.py:477
  26.0 16.0 %collective-permute-start.10 = (bf16[384,128]{1,0:T(8,128)(2,1)S(1)}, bf16[384,128]{1,0:T(8,128)(2,1)S(1)}, u32[]{:S(2)}, u32[]{:S(2)}) collective-permute-start(bf16[384,128]{1,0:T(8,128)(2,1)S(1)} %get-tuple-element.79), channel_id=1, source_target_pairs={{0,4},{4,0},{8,12},{12,8},{1,5},{5,1},{9,13},{13,9},{2,6},{6,2},{1... | collective-permute-start | bytes 294920 | tf_op jit(solution)/shard_map/ppermute | solution.py:399
  34.6 10.0 %collective-permute-start.11 = (bf16[384,128]{1,0:T(8,128)(2,1)S(1)}, bf16[384,128]{1,0:T(8,128)(2,1)S(1)}, u32[]{:S(2)}, u32[]{:S(2)}) collective-permute-start(bf16[384,128]{1,0:T(8,128)(2,1)S(1)} %get-tuple-element.78), channel_id=1, source_target_pairs={{0,8},{4,12},{8,0},{12,4},{1,9},{5,13},{9,1},{13,5},{2,10},{6,14},... | collective-permute-start | bytes 294920 | tf_op jit(solution)/shard_map/ppermute | solution.py:399
  35.7 8.9 %collective-permute-start.12 = (bf16[384,128]{1,0:T(8,128)(2,1)S(1)}, bf16[384,128]{1,0:T(8,128)(2,1)S(1)}, u32[]{:S(2)}, u32[]{:S(2)}) collective-permute-start(bf16[384,128]{1,0:T(8,128)(2,1)S(1)} %get-tuple-element.77), channel_id=1, source_target_pairs={{0,12},{4,8},{8,4},{12,0},{1,13},{5,9},{9,5},{13,1},{2,14},{6,10},... | collective-permute-start | bytes 294920 | tf_op jit(solution)/shard_map/ppermute | solution.py:399
  37.1 12.7 %collective-permute-start.6 = (bf16[512,128]{1,0:T(8,128)(2,1)S(1)}, bf16[512,128]{1,0:T(8,128)(2,1)S(1)}, u32[]{:S(2)}, u32[]{:S(2)}) collective-permute-start(bf16[512,128]{1,0:T(8,128)(2,1)S(1)} %get-tuple-element.51), channel_id=1, source_target_pairs={{0,1},{1,0},{2,3},{3,2},{4,5},{5,4},{6,7},{7,6},{8,9},{9,8},{10,11... | collective-permute-start | bytes 393224 | tf_op jit(solution)/shard_map/ppermute | solution.py:399
  42.0 10.3 %collective-permute-start.7 = (bf16[512,128]{1,0:T(8,128)(2,1)S(1)}, bf16[512,128]{1,0:T(8,128)(2,1)S(1)}, u32[]{:S(2)}, u32[]{:S(2)}) collective-permute-start(bf16[512,128]{1,0:T(8,128)(2,1)S(1)} %get-tuple-element.50.mine), channel_id=1, source_target_pairs={{0,2},{2,0},{1,3},{3,1},{4,6},{6,4},{5,7},{7,5},{8,10},{10,8},{9,1... | collective-permute-start | bytes 393224 | tf_op jit(solution)/shard_map/ppermute | solution.py:399
  45.2 7.1 %collective-permute-start.14 = (bf16[384,128]{1,0:T(8,128)(2,1)S(1)}, bf16[384,128]{1,0:T(8,128)(2,1)S(1)}, u32[]{:S(2)}, u32[]{:S(2)}) collective-permute-start(bf16[384,128]{1,0:T(8,128)(2,1)S(1)} %shard_map.110), channel_id=1, source_target_pairs={{0,4},{4,0},{8,12},{12,8},{1,5},{5,1},{9,13},{13,9},{2,6},{6,2},{1... | collective-permute-start | bytes 294920 | tf_op jit(solution)/shard_map/ppermute | solution.py:399
  47.3 9.4 %collective-permute-start.15 = (bf16[384,128]{1,0:T(8,128)(2,1)S(1)}, bf16[384,128]{1,0:T(8,128)(2,1)S(1)}, u32[]{:S(2)}, u32[]{:S(2)}) collective-permute-start(bf16[384,128]{1,0:T(8,128)(2,1)S(1)} %shard_map.110), channel_id=1, source_target_pairs={{0,8},{4,12},{8,0},{12,4},{1,9},{5,13},{9,1},{13,5},{2,10},{6,14},... | collective-permute-start | bytes 294920 | tf_op jit(solution)/shard_map/ppermute | solution.py:399
  48.2 8.5 %collective-permute-start.16 = (bf16[384,128]{1,0:T(8,128)(2,1)S(1)}, bf16[384,128]{1,0:T(8,128)(2,1)S(1)}, u32[]{:S(2)}, u32[]{:S(2)}) collective-permute-start(bf16[384,128]{1,0:T(8,128)(2,1)S(1)} %shard_map.110), channel_id=1, source_target_pairs={{0,12},{4,8},{8,4},{12,0},{1,13},{5,9},{9,5},{13,1},{2,14},{6,10},... | collective-permute-start | bytes 294920 | tf_op jit(solution)/shard_map/ppermute | solution.py:399
  49.8 7.0 %collective-permute-start.8 = (bf16[512,128]{1,0:T(8,128)(2,1)S(1)}, bf16[512,128]{1,0:T(8,128)(2,1)S(1)}, u32[]{:S(2)}, u32[]{:S(2)}) collective-permute-start(bf16[512,128]{1,0:T(8,128)(2,1)S(1)} %collective-permute-done.6.rep), channel_id=1, source_target_pairs={{0,2},{2,0},{1,3},{3,1},{4,6},{6,4},{5,7},{7,5},{8,10},{10,8},{9,1... | collective-permute-start | bytes 393224 | tf_op jit(solution)/shard_map/ppermute | solution.py:399
  58.8 5.8 %collective-permute-start.17 = (bf16[512,512]{1,0:T(8,128)(2,1)S(1)}, bf16[512,512]{1,0:T(8,128)(2,1)S(1)}, u32[]{:S(2)}, u32[]{:S(2)}) collective-permute-start(bf16[512,512]{1,0:T(8,128)(2,1)S(1)} %get-tuple-element.61), channel_id=1, source_target_pairs={{0,1},{1,0},{2,3},{3,2},{4,5},{5,4},{6,7},{7,6},{8,9},{9,8},{10,11... | collective-permute-start | bytes 1572872 | tf_op jit(solution)/shard_map/ppermute | solution.py:399
  58.9 7.7 %collective-permute-start.19 = (bf16[1536,128]{1,0:T(8,128)(2,1)S(1)}, bf16[1536,128]{1,0:T(8,128)(2,1)S(1)}, u32[]{:S(2)}, u32[]{:S(2)}) collective-permute-start(bf16[1536,128]{1,0:T(8,128)(2,1)S(1)} %pad_maximum_fusion.refs_0_), channel_id=1, source_target_pairs={{0,1},{1,0},{2,3},{3,2},{4,5},{5,4},{6,7},{7,6},{8,9},{9,8},{10,11... | collective-permute-start | bytes 1179656 | tf_op jit(solution)/shard_map/ppermute | solution.py:399
  60.0 9.1 %collective-permute-start.20 = (bf16[272,128]{1,0:T(8,128)(2,1)S(1)}, bf16[272,128]{1,0:T(8,128)(2,1)S(1)}, u32[]{:S(2)}, u32[]{:S(2)}) collective-permute-start(bf16[272,128]{1,0:T(8,128)(2,1)S(1)} %get-tuple-element.83), channel_id=1, source_target_pairs={{0,4},{4,0},{8,12},{12,8},{1,5},{5,1},{9,13},{13,9},{2,6},{6,2},{1... | collective-permute-start | bytes 208904 | tf_op jit(solution)/shard_map/ppermute | solution.py:399
  62.1 8.3 %collective-permute-start.21 = (bf16[272,128]{1,0:T(8,128)(2,1)S(1)}, bf16[272,128]{1,0:T(8,128)(2,1)S(1)}, u32[]{:S(2)}, u32[]{:S(2)}) collective-permute-start(bf16[272,128]{1,0:T(8,128)(2,1)S(1)} %get-tuple-element.82), channel_id=1, source_target_pairs={{0,8},{4,12},{8,0},{12,4},{1,9},{5,13},{9,1},{13,5},{2,10},{6,14},... | collective-permute-start | bytes 208904 | tf_op jit(solution)/shard_map/ppermute | solution.py:399
  62.5 7.9 %collective-permute-start.22 = (bf16[272,128]{1,0:T(8,128)(2,1)S(1)}, bf16[272,128]{1,0:T(8,128)(2,1)S(1)}, u32[]{:S(2)}, u32[]{:S(2)}) collective-permute-start(bf16[272,128]{1,0:T(8,128)(2,1)S(1)} %get-tuple-element.81), channel_id=1, source_target_pairs={{0,12},{4,8},{8,4},{12,0},{1,13},{5,9},{9,5},{13,1},{2,14},{6,10},... | collective-permute-start | bytes 208904 | tf_op jit(solution)/shard_map/ppermute | solution.py:399
  65.3 13.9 %collective-permute-start.18 = (bf16[512,512]{1,0:T(8,128)(2,1)S(1)}, bf16[512,512]{1,0:T(8,128)(2,1)S(1)}, u32[]{:S(2)}, u32[]{:S(2)}) collective-permute-start(bf16[512,512]{1,0:T(8,128)(2,1)S(1)} %shard_map.112.mine), channel_id=1, source_target_pairs={{0,2},{2,0},{1,3},{3,1},{4,6},{6,4},{5,7},{7,5},{8,10},{10,8},{9,1... | collective-permute-start | bytes 1572872 | tf_op jit(solution)/shard_map/ppermute | solution.py:399
  71.0 10.2 %collective-permute-start.24 = (bf16[256,128]{1,0:T(8,128)(2,1)S(1)}, bf16[256,128]{1,0:T(8,128)(2,1)S(1)}, u32[]{:S(2)}, u32[]{:S(2)}) collective-permute-start(bf16[256,128]{1,0:T(8,128)(2,1)S(1)} %get-tuple-element.70.refs_0_), channel_id=1, source_target_pairs={{0,4},{4,0},{8,12},{12,8},{1,5},{5,1},{9,13},{13,9},{2,6},{6,2},{1... | collective-permute-start | bytes 196616 | tf_op jit(solution)/shard_map/ppermute | solution.py:399
  72.5 8.8 %collective-permute-start.25 = (bf16[256,128]{1,0:T(8,128)(2,1)S(1)}, bf16[256,128]{1,0:T(8,128)(2,1)S(1)}, u32[]{:S(2)}, u32[]{:S(2)}) collective-permute-start(bf16[256,128]{1,0:T(8,128)(2,1)S(1)} %get-tuple-element.70.refs_0_), channel_id=1, source_target_pairs={{0,8},{4,12},{8,0},{12,4},{1,9},{5,13},{9,1},{13,5},{2,10},{6,14},... | collective-permute-start | bytes 196616 | tf_op jit(solution)/shard_map/ppermute | solution.py:399
  73.2 8.0 %collective-permute-start.26 = (bf16[256,128]{1,0:T(8,128)(2,1)S(1)}, bf16[256,128]{1,0:T(8,128)(2,1)S(1)}, u32[]{:S(2)}, u32[]{:S(2)}) collective-permute-start(bf16[256,128]{1,0:T(8,128)(2,1)S(1)} %get-tuple-element.70.refs_0_), channel_id=1, source_target_pairs={{0,12},{4,8},{8,4},{12,0},{1,13},{5,9},{9,5},{13,1},{2,14},{6,10},... | collective-permute-start | bytes 196616 | tf_op jit(solution)/shard_map/ppermute | solution.py:399
  75.5 3.7 %collective-permute-start.23 = (f32[1,512]{1,0:T(1,128)S(1)}, f32[1,512]{1,0:T(1,128)S(1)}, u32[]{:S(2)}, u32[]{:S(2)}) collective-permute-start(f32[1,512]{1,0:T(1,128)S(1)} %get-tuple-element.66.pg_a), channel_id=1, source_target_pairs={{0,2},{2,0},{1,3},{3,1},{4,6},{6,4},{5,7},{7,5},{8,10},{10,8},{9,1... | collective-permute-start | bytes 6152 | tf_op jit(solution)/shard_map/ppermute | solution.py:399
  81.2 2.2 %collective-permute-start.27 = (bf16[256,128]{1,0:T(8,128)(2,1)S(1)}, bf16[256,128]{1,0:T(8,128)(2,1)S(1)}, u32[]{:S(2)}, u32[]{:S(2)}) collective-permute-start(bf16[256,128]{1,0:T(8,128)(2,1)S(1)} %get-tuple-element.70.refs_0_), channel_id=1, source_target_pairs={{0,1},{1,0},{2,3},{3,2},{4,5},{5,4},{6,7},{7,6},{8,9},{9,8},{10,11... | collective-permute-start | bytes 196616 | tf_op jit(solution)/shard_map/ppermute | solution.py:399
  81.3 2.2 %collective-permute-start.28 = (bf16[256,128]{1,0:T(8,128)(2,1)S(1)}, bf16[256,128]{1,0:T(8,128)(2,1)S(1)}, u32[]{:S(2)}, u32[]{:S(2)}) collective-permute-start(bf16[256,128]{1,0:T(8,128)(2,1)S(1)} %collective-permute-done.24.refs_1_), channel_id=1, source_target_pairs={{0,1},{1,0},{2,3},{3,2},{4,5},{5,4},{6,7},{7,6},{8,9},{9,8},{10,11... | collective-permute-start | bytes 196616 | tf_op jit(solution)/shard_map/ppermute | solution.py:399
  81.8 1.7 %collective-permute-start.29 = (bf16[256,128]{1,0:T(8,128)(2,1)S(1)}, bf16[256,128]{1,0:T(8,128)(2,1)S(1)}, u32[]{:S(2)}, u32[]{:S(2)}) collective-permute-start(bf16[256,128]{1,0:T(8,128)(2,1)S(1)} %collective-permute-done.25.refs_2_), channel_id=1, source_target_pairs={{0,1},{1,0},{2,3},{3,2},{4,5},{5,4},{6,7},{7,6},{8,9},{9,8},{10,11... | collective-permute-start | bytes 196616 | tf_op jit(solution)/shard_map/ppermute | solution.py:399
  81.9 1.6 %collective-permute-start.30 = (bf16[256,128]{1,0:T(8,128)(2,1)S(1)}, bf16[256,128]{1,0:T(8,128)(2,1)S(1)}, u32[]{:S(2)}, u32[]{:S(2)}) collective-permute-start(bf16[256,128]{1,0:T(8,128)(2,1)S(1)} %collective-permute-done.26.refs_3_), channel_id=1, source_target_pairs={{0,1},{1,0},{2,3},{3,2},{4,5},{5,4},{6,7},{7,6},{8,9},{9,8},{10,11... | collective-permute-start | bytes 196616 | tf_op jit(solution)/shard_map/ppermute | solution.py:399
  82.3 1.2 %collective-permute-start.31 = (f32[1,512]{1,0:T(1,128)S(1)}, f32[1,512]{1,0:T(1,128)S(1)}, u32[]{:S(2)}, u32[]{:S(2)}) collective-permute-start(f32[1,512]{1,0:T(1,128)S(1)} %get-tuple-element.69.refs_8_), channel_id=1, source_target_pairs={{0,1},{1,0},{2,3},{3,2},{4,5},{5,4},{6,7},{7,6},{8,9},{9,8},{10,11... | collective-permute-start | bytes 6152 | tf_op jit(solution)/shard_map/ppermute | solution.py:399
  (6 other events, 35.3 us)
